TPU v7x, 128 devices: a whole 4x4x4 slice. The times are simulated.
128 devices in a mesh: ctx: 16 (over y, x_lo, core), section: 8 (over z, x_hi).
Axes of the slice: x: 4 (x_hi: 2, x_lo: 2; x = x_hi * 2 + x_lo), y: 4, z: 4, core: 2. Of those that a mesh axis runs over, the one named last changes fastest.
Arguments:
- x_saved: bfloat16 [8, 2048, 4096], P('section', 'ctx'), may hold values from -400 to 400
- gains: float32 [8, 4096], P('section'), may hold values from 0.5 to 2
- keys: bfloat16 [2048, 4096], P(('ctx', 'section')), may hold values from -18 to 18
- values: bfloat16 [2048, 4096], P(('ctx', 'section')), may hold values from -6 to 6
- grad_top: bfloat16 [2048, 4096], P('ctx'), may hold values from -6 to 6
- block_order: int32 [16], replicated, may hold values from 0 to 15, each once
Outputs:
- grad_inputs: float32 [8, 2048, 4096], P('section', 'ctx')
- grad_keys: float32 [2048, 4096], P(('ctx', 'section'))
- grad_values: float32 [2048, 4096], P(('ctx', 'section'))
Inputs may be any that keep to these rules, and one draw needn't show every extreme that they name: `block_order`: each place occurs once.
All inputs are finite; a program needn't handle non-finite values.
Results may differ from a plain program's by a relative error of at most 0.015.
The roundings to bfloat16 on the way count: a program that leaves them out, or rounds other values in their place, can miss the bound.
Values may be sent and summed in bfloat16 or wider, within the bound.
A program may use at most 128 MiB of HBM per device.

v0:
```python
import math

import jax
import jax.numpy as jnp
from jax import lax
from jax.sharding import PartitionSpec as P

H = 32
HD = 128


masked_score = -1e30
norm_eps = 1e-06


def passed_along(value, axis, steps):
    count = lax.axis_size(axis)
    first, last = (max(0, -steps), min(count, count - steps))
    return lax.ppermute(value, axis, [(source, source + steps) for source in range(first, last)])


def make_query(inputs, gain_row):
    x_float = inputs.astype(jnp.float32).reshape(inputs.shape[0], H, HD)
    inv_rms = lax.rsqrt(jnp.mean(x_float * x_float, axis=-1, keepdims=True) + norm_eps)
    queries = x_float * inv_rms * gain_row.reshape(H, HD)
    return (queries, x_float, inv_rms)


def input_grad(query_grads, x_float, inv_rms, gain_row):
    scaled = query_grads * gain_row.reshape(H, HD)
    inner = jnp.mean(scaled * x_float, axis=-1, keepdims=True)
    result = inv_rms * scaled - x_float * (inv_rms * inv_rms * inv_rms) * inner
    return result.reshape(query_grads.shape[0], H * HD)


def attend_block(query_heads, grad_heads, keys_heads, values_heads, query_places, key_places):
    factor = 1.0 / math.sqrt(HD)
    scores = (
        jnp.einsum("qhd,khd->hqk", query_heads, keys_heads, preferred_element_type=jnp.float32)
        * factor
    )
    visible = query_places[:, None] >= key_places[None, :]
    scores = jnp.where(visible[None], scores, masked_score)
    row_max = jnp.max(scores, axis=-1, keepdims=True)
    probs = jnp.exp(scores - row_max)
    probs = probs / jnp.sum(probs, axis=-1, keepdims=True)
    probs_low = probs.astype(jnp.bfloat16)
    recomputed = jnp.einsum(
        "hqk,khd->qhd", probs_low, values_heads, preferred_element_type=jnp.float32
    )
    row_delta = jnp.sum(grad_heads.astype(jnp.float32) * recomputed, axis=-1)
    dprobs = jnp.einsum(
        "qhd,khd->hqk", grad_heads, values_heads, preferred_element_type=jnp.float32
    )
    dscores = (probs * (dprobs - jnp.transpose(row_delta)[:, :, None])).astype(jnp.bfloat16)
    query_grad = (
        jnp.einsum("hqk,khd->qhd", dscores, keys_heads, preferred_element_type=jnp.float32) * factor
    )
    key_part = (
        jnp.einsum("hqk,qhd->khd", dscores, query_heads, preferred_element_type=jnp.float32)
        * factor
    )
    value_part = jnp.einsum(
        "hqk,qhd->khd", probs_low, grad_heads, preferred_element_type=jnp.float32
    )
    return (query_grad, key_part, value_part)


def body(x_saved, gains, keys, values, grad_top, block_order):
    ctx_count = lax.axis_size("ctx")
    section_count = lax.axis_size("section")
    section_id = lax.axis_index("section")
    tok_dev = x_saved.shape[1]
    width = x_saved.shape[2]
    local_heads = H // ctx_count
    local_width = local_heads * HD
    all_tokens = tok_dev * ctx_count
    full_keys, full_values = (
        lax.all_gather(keys, "section", axis=0, tiled=True),
        lax.all_gather(values, "section", axis=0, tiled=True),
    )
    keys_heads, values_heads = (
        lax.all_to_all(
            full_keys.reshape(tok_dev, ctx_count, local_width),
            "ctx",
            split_axis=1,
            concat_axis=0,
            tiled=True,
        ),
        lax.all_to_all(
            full_values.reshape(tok_dev, ctx_count, local_width),
            "ctx",
            split_axis=1,
            concat_axis=0,
            tiled=True,
        ),
    )
    keys_heads = keys_heads.reshape(all_tokens, local_heads, HD)
    values_heads = values_heads.reshape(all_tokens, local_heads, HD)
    key_places = (
        block_order[:, None] * tok_dev + jnp.arange(tok_dev, dtype=jnp.int32)[None, :]
    ).reshape(all_tokens)
    blocks = 4
    block_rows = tok_dev // blocks
    turn_count = section_count - 1 + blocks
    top_grad = grad_top.astype(jnp.float32)
    x_local = x_saved[0]
    gain_row = gains[0]
    section_lag = section_count - 1 - section_id

    def one_turn(turn_step, state_in):
        received, collected, key_sum, value_sum = state_in
        turn_index = turn_step - section_lag
        is_valid = (turn_index >= 0) & (turn_index < blocks)
        row_block = jnp.clip(turn_index, 0, blocks - 1)
        from_top = lax.dynamic_slice_in_dim(
            top_grad, jnp.clip(turn_step, 0, blocks - 1) * block_rows, block_rows, 0
        )
        incoming = jnp.where(section_id == section_count - 1, from_top, received)
        incoming = jnp.where(is_valid, incoming, 0.0)
        x_rows = lax.dynamic_slice_in_dim(x_local, row_block * block_rows, block_rows, 0)
        queries, x_float, inv_rms = make_query(x_rows, gain_row)
        outgoing = (
            queries.astype(jnp.bfloat16).reshape(block_rows, ctx_count, local_width),
            incoming.astype(jnp.bfloat16).reshape(block_rows, ctx_count, local_width),
        )
        query_heads, grad_heads = (
            lax.all_to_all(outgoing[0], "ctx", split_axis=1, concat_axis=0, tiled=True),
            lax.all_to_all(outgoing[1], "ctx", split_axis=1, concat_axis=0, tiled=True),
        )
        query_heads = query_heads.reshape(ctx_count * block_rows, local_heads, HD)
        grad_heads = grad_heads.reshape(ctx_count * block_rows, local_heads, HD)
        query_places = (
            block_order[:, None] * tok_dev
            + row_block * block_rows
            + jnp.arange(block_rows, dtype=jnp.int32)[None, :]
        ).reshape(ctx_count * block_rows)
        query_grad, key_part, value_part = attend_block(
            query_heads, grad_heads, keys_heads, values_heads, query_places, key_places
        )
        returned = lax.all_to_all(
            query_grad.reshape(ctx_count * block_rows, 1, local_width),
            "ctx",
            split_axis=0,
            concat_axis=1,
            tiled=True,
        )
        branch = input_grad(returned.reshape(block_rows, H, HD), x_float, inv_rms, gain_row)
        leaving = jnp.where(is_valid, incoming + branch, 0.0)
        old_rows = lax.dynamic_slice_in_dim(collected, row_block * block_rows, block_rows, 0)
        collected = lax.dynamic_update_slice_in_dim(
            collected, jnp.where(is_valid, leaving, old_rows), row_block * block_rows, 0
        )
        received = passed_along(leaving, "section", -1)
        return (received, collected, key_sum + key_part, value_sum + value_part)

    start_state = (
        jnp.zeros((block_rows, width), jnp.float32),
        jnp.zeros((tok_dev, width), jnp.float32),
        jnp.zeros((all_tokens, local_heads, HD), jnp.float32),
        jnp.zeros((all_tokens, local_heads, HD), jnp.float32),
    )
    received, collected, key_sum, value_sum = lax.fori_loop(0, turn_count, one_turn, start_state)
    token_keys, token_values = (
        lax.all_to_all(
            key_sum.reshape(all_tokens, 1, local_width).astype(jnp.bfloat16),
            "ctx",
            split_axis=0,
            concat_axis=1,
            tiled=True,
        ).astype(jnp.float32),
        lax.all_to_all(
            value_sum.reshape(all_tokens, 1, local_width).astype(jnp.bfloat16),
            "ctx",
            split_axis=0,
            concat_axis=1,
            tiled=True,
        ).astype(jnp.float32),
    )
    grad_keys, grad_values = (
        lax.psum_scatter(
            token_keys.reshape(tok_dev, width).astype(jnp.bfloat16),
            "section",
            scatter_dimension=0,
            tiled=True,
        ).astype(jnp.float32),
        lax.psum_scatter(
            token_values.reshape(tok_dev, width).astype(jnp.bfloat16),
            "section",
            scatter_dimension=0,
            tiled=True,
        ).astype(jnp.float32),
    )
    return (collected[None], grad_keys, grad_values)


def solution(mesh):
    placed = (
        P("section", "ctx", None),
        P("section", None),
        P(("ctx", "section"), None),
        P(("ctx", "section"), None),
        P("ctx", None),
        P(),
    )
    return jax.shard_map(
        body,
        mesh=mesh,
        in_specs=placed,
        out_specs=(
            P("section", "ctx", None),
            P(("ctx", "section"), None),
            P(("ctx", "section"), None),
        ),
        check_vma=False,
    )
```

profile of v0, /device:TPU:1, one launch (start us, length us, event | category | flops | bytes accessed | tf_op | source)
XLA Modules:
  0.0 1218.0 jit_solution(8737538382980565483)
XLA Ops:
  8.7 50.1 %all-gather.5.cloned.1.call-done = bf16[128,4096]{1,0:T(8,128)(2,1)} async-done(((bf16[16,4096]{1,0:T(8,128)(2,1)}), bf16[128,4096]{1,0:T(8,128)(2,1)}) %all-gather.5.cloned.1.call-update) | async-done | bytes 1048592 | tf_op jit(solution)/shard_map/all_gather | solution.py:80
  67.3 40.6 %all-gather.3.cloned.1.call-done = bf16[128,4096]{1,0:T(8,128)(2,1)} async-done(((bf16[16,4096]{1,0:T(8,128)(2,1)}), bf16[128,4096]{1,0:T(8,128)(2,1)}) %all-gather.3.cloned.1.call-update) | async-done | bytes 1048592 | tf_op jit(solution)/shard_map/all_gather | solution.py:79
  119.9 12.2 %all-to-all-done.3 = bf16[128,16,256]{0,2,1:T(8,128)(2,1)S(1)} async-done(((bf16[128,16,256]{0,2,1:T(8,128)(2,1)}), bf16[128,16,256]{0,2,1:T(8,128)(2,1)S(1)}, u32[]{:S(2)}, u32[]{:S(2)}) %all-to-all-start.3) | async-done | bytes 1048608 | tf_op jit(solution)/shard_map/all_to_all | solution.py:83
  135.7 895.3 %while.22 = (s32[]{:T(128)}, f32[32,4096]{1,0:T(8,128)S(1)}, f32[128,4096]{1,0:T(8,128)}, f32[2048,2,128]{0,2,1:T(8,128)}, f32[2048,2,128]{0,2,1:T(8,128)}, /*in...) while((s32[]{:T(128)}, f32[32,4096]{1,0:T(8,128)S(1)}, ...), condition=%wide.region_6.7_spmd.clone, body=%wide.region_0.6_spmd.clone.sunk | while | flops 3249281536 | bytes 240326320 | solution.py:163
  160.9 6.5 fusion.70
  184.8 9.9 all-to-all-done.2
  205.7 9.5 collective-permute-done
  241.7 6.5 fusion.70
  265.6 9.9 all-to-all-done.2
  286.5 9.5 collective-permute-done
  346.3 9.9 all-to-all-done.2
  367.2 10.5 collective-permute-done
  427.7 9.9 all-to-all-done.2
  448.6 10.7 collective-permute-done
  509.4 9.9 all-to-all-done.2
  530.3 10.7 collective-permute-done
  591.1 9.9 all-to-all-done.2
  612.0 10.7 collective-permute-done
  672.7 9.9 all-to-all-done.2
  693.6 10.7 collective-permute-done
  754.4 9.9 all-to-all-done.2
  775.3 10.7 collective-permute-done
  836.1 9.9 all-to-all-done.2
  857.0 10.7 collective-permute-done
  917.7 9.9 all-to-all-done.2
  938.6 10.7 collective-permute-done
  999.4 9.9 all-to-all-done.2
  1020.3 10.7 collective-permute-done
  1035.5 19.7 %all_to_all.177 = bf16[16,2,16384]{2,1,0:T(2,128)(2,1)S(1)} all-to-all(bf16[16,2,16384]{2,1,0:T(2,128)(2,1)S(1)} %reshape.291), channel_id=1, replica_groups=mesh['ctx'=16,'section'=8] {'ctx'}, dimensions={0} | all-to-all | bytes 2097152 | tf_op jit(solution)/shard_map/all_to_all | solution.py:165
  1066.7 20.5 %all_to_all.178 = bf16[16,2,16384]{2,1,0:T(2,128)(2,1)S(1)} all-to-all(bf16[16,2,16384]{2,1,0:T(2,128)(2,1)S(1)} %reshape.293), channel_id=1, replica_groups=mesh['ctx'=16,'section'=8] {'ctx'}, dimensions={0} | all-to-all | bytes 2097152 | tf_op jit(solution)/shard_map/all_to_all | solution.py:172
  1090.5 44.0 %reduce-scatter.7.cloned.1.call-done = bf16[16,4096]{1,0:T(8,128)(2,1)} async-done(((bf16[128,4096]{1,0:T(8,128)(2,1)}), bf16[16,4096]{1,0:T(8,128)(2,1)}) %reduce-scatter.7.cloned.1.call-update) | async-done | bytes 131088
  1136.9 72.1 %reduce-scatter.9.cloned.1.call-done = bf16[16,4096]{1,0:T(8,128)(2,1)} async-done(((bf16[128,4096]{1,0:T(8,128)(2,1)}), bf16[16,4096]{1,0:T(8,128)(2,1)}) %reduce-scatter.9.cloned.1.call-update) | async-done | bytes 131088
  (831 shorter events, 703.7 us)
Async XLA Ops:
  7.2 51.6 %all-gather.5.cloned.1.call-start = ((), (), s32[]{:S(2)}) async-start(), calls=%async_computation.10 | async-start | bytes 1179648 | tf_op jit(solution)/shard_map/all_gather | solution.py:80
  7.9 100.0 %all-gather.3.cloned.1.call-start = ((), (), s32[]{:S(2)}) async-start(), calls=%async_computation.9 | async-start | bytes 1179648 | tf_op jit(solution)/shard_map/all_gather | solution.py:79
  61.1 49.0 %all-to-all-start.4 = ((bf16[128,16,256]{0,2,1:T(8,128)(2,1)}), bf16[128,16,256]{0,2,1:T(8,128)(2,1)S(1)}, u32[]{:S(2)}, u32[]{:S(2)}) async-start(bf16[128,16,256]{0,2,1:T(8,128)(2,1)} %bitcast.4), calls=%async_computation.4 | async-start | bytes 2097152 | tf_op jit(solution)/shard_map/all_to_all | solution.py:90
  110.1 22.0 %all-to-all-start.3 = ((bf16[128,16,256]{0,2,1:T(8,128)(2,1)}), bf16[128,16,256]{0,2,1:T(8,128)(2,1)S(1)}, u32[]{:S(2)}, u32[]{:S(2)}) async-start(bf16[128,16,256]{0,2,1:T(8,128)(2,1)} %bitcast.1), calls=%async_computation.3 | async-start | bytes 2097152 | tf_op jit(solution)/shard_map/all_to_all | solution.py:83
  116.3 1018.2 %reduce-scatter.7.cloned.1.call-start = ((), (), s32[]{:S(2)}) async-start(), calls=%async_computation.11 | async-start | bytes 1179648
  180.5 14.2 %all-to-all-start.2 = ((f32[512,1,256]{2,1,0:T(1,128)}), f32[512,1,256]{2,1,0:T(1,128)S(1)}, u32[]{:S(2)}, u32[]{:S(2)}) async-start(f32[512,1,256]{2,1,0:T(1,128)} %copy.136), calls=%async_computation.2 | async-start | bytes 1048576 | tf_op jit(solution)/shard_map/while/body/eval_jaxpr/all_to_all | solution.py:141
  199.6 15.6 %collective-permute-start = (f32[32,4096]{1,0:T(8,128)S(1)}, f32[32,4096]{1,0:T(8,128)S(1)}, u32[]{:S(2)}, u32[]{:S(2)}) collective-permute-start(f32[32,4096]{1,0:T(8,128)S(1)} %get-tuple-element.520), channel_id=1, source_target_pairs={{1,0},{2,1},{3,2},{4,3},{5,4},{6,5},{7,6},{9,8},{10,9},{11,10},{12... | collective-permute-start | bytes 1572872 | tf_op jit(solution)/shard_map/while/body/eval_jaxpr/ppermute | solution.py:19
  217.2 12.6 %all-to-all-start = ((bf16[32,16,256]{2,0,1:T(8,128)(2,1)}), bf16[32,16,256]{2,0,1:T(8,128)(2,1)S(1)}, u32[]{:S(2)}, u32[]{:S(2)}) async-start(bf16[32,16,256]{2,0,1:T(8,128)(2,1)} %bitcast.181), calls=%async_computation | async-start | bytes 524288 | tf_op jit(solution)/shard_map/while/body/eval_jaxpr/all_to_all | solution.py:129
  261.2 14.2 %all-to-all-start.2 = ((f32[512,1,256]{2,1,0:T(1,128)}), f32[512,1,256]{2,1,0:T(1,128)S(1)}, u32[]{:S(2)}, u32[]{:S(2)}) async-start(f32[512,1,256]{2,1,0:T(1,128)} %copy.136), calls=%async_computation.2 | async-start | bytes 1048576 | tf_op jit(solution)/shard_map/while/body/eval_jaxpr/all_to_all | solution.py:141
  280.4 15.6 %collective-permute-start = (f32[32,4096]{1,0:T(8,128)S(1)}, f32[32,4096]{1,0:T(8,128)S(1)}, u32[]{:S(2)}, u32[]{:S(2)}) collective-permute-start(f32[32,4096]{1,0:T(8,128)S(1)} %get-tuple-element.520), channel_id=1, source_target_pairs={{1,0},{2,1},{3,2},{4,3},{5,4},{6,5},{7,6},{9,8},{10,9},{11,10},{12... | collective-permute-start | bytes 1572872 | tf_op jit(solution)/shard_map/while/body/eval_jaxpr/ppermute | solution.py:19
  298.0 12.6 %all-to-all-start = ((bf16[32,16,256]{2,0,1:T(8,128)(2,1)}), bf16[32,16,256]{2,0,1:T(8,128)(2,1)S(1)}, u32[]{:S(2)}, u32[]{:S(2)}) async-start(bf16[32,16,256]{2,0,1:T(8,128)(2,1)} %bitcast.181), calls=%async_computation | async-start | bytes 524288 | tf_op jit(solution)/shard_map/while/body/eval_jaxpr/all_to_all | solution.py:129
  342.0 14.2 %all-to-all-start.2 = ((f32[512,1,256]{2,1,0:T(1,128)}), f32[512,1,256]{2,1,0:T(1,128)S(1)}, u32[]{:S(2)}, u32[]{:S(2)}) async-start(f32[512,1,256]{2,1,0:T(1,128)} %copy.136), calls=%async_computation.2 | async-start | bytes 1048576 | tf_op jit(solution)/shard_map/while/body/eval_jaxpr/all_to_all | solution.py:141
  361.1 16.6 %collective-permute-start = (f32[32,4096]{1,0:T(8,128)S(1)}, f32[32,4096]{1,0:T(8,128)S(1)}, u32[]{:S(2)}, u32[]{:S(2)}) collective-permute-start(f32[32,4096]{1,0:T(8,128)S(1)} %get-tuple-element.520), channel_id=1, source_target_pairs={{1,0},{2,1},{3,2},{4,3},{5,4},{6,5},{7,6},{9,8},{10,9},{11,10},{12... | collective-permute-start | bytes 1572872 | tf_op jit(solution)/shard_map/while/body/eval_jaxpr/ppermute | solution.py:19
  379.7 12.3 %all-to-all-start = ((bf16[32,16,256]{2,0,1:T(8,128)(2,1)}), bf16[32,16,256]{2,0,1:T(8,128)(2,1)S(1)}, u32[]{:S(2)}, u32[]{:S(2)}) async-start(bf16[32,16,256]{2,0,1:T(8,128)(2,1)} %bitcast.181), calls=%async_computation | async-start | bytes 524288 | tf_op jit(solution)/shard_map/while/body/eval_jaxpr/all_to_all | solution.py:129
  423.4 14.2 %all-to-all-start.2 = ((f32[512,1,256]{2,1,0:T(1,128)}), f32[512,1,256]{2,1,0:T(1,128)S(1)}, u32[]{:S(2)}, u32[]{:S(2)}) async-start(f32[512,1,256]{2,1,0:T(1,128)} %copy.136), calls=%async_computation.2 | async-start | bytes 1048576 | tf_op jit(solution)/shard_map/while/body/eval_jaxpr/all_to_all | solution.py:141
  442.5 16.8 %collective-permute-start = (f32[32,4096]{1,0:T(8,128)S(1)}, f32[32,4096]{1,0:T(8,128)S(1)}, u32[]{:S(2)}, u32[]{:S(2)}) collective-permute-start(f32[32,4096]{1,0:T(8,128)S(1)} %get-tuple-element.520), channel_id=1, source_target_pairs={{1,0},{2,1},{3,2},{4,3},{5,4},{6,5},{7,6},{9,8},{10,9},{11,10},{12... | collective-permute-start | bytes 1572872 | tf_op jit(solution)/shard_map/while/body/eval_jaxpr/ppermute | solution.py:19
  461.3 12.3 %all-to-all-start = ((bf16[32,16,256]{2,0,1:T(8,128)(2,1)}), bf16[32,16,256]{2,0,1:T(8,128)(2,1)S(1)}, u32[]{:S(2)}, u32[]{:S(2)}) async-start(bf16[32,16,256]{2,0,1:T(8,128)(2,1)} %bitcast.181), calls=%async_computation | async-start | bytes 524288 | tf_op jit(solution)/shard_map/while/body/eval_jaxpr/all_to_all | solution.py:129
  505.0 14.2 %all-to-all-start.2 = ((f32[512,1,256]{2,1,0:T(1,128)}), f32[512,1,256]{2,1,0:T(1,128)S(1)}, u32[]{:S(2)}, u32[]{:S(2)}) async-start(f32[512,1,256]{2,1,0:T(1,128)} %copy.136), calls=%async_computation.2 | async-start | bytes 1048576 | tf_op jit(solution)/shard_map/while/body/eval_jaxpr/all_to_all | solution.py:141
  524.2 16.8 %collective-permute-start = (f32[32,4096]{1,0:T(8,128)S(1)}, f32[32,4096]{1,0:T(8,128)S(1)}, u32[]{:S(2)}, u32[]{:S(2)}) collective-permute-start(f32[32,4096]{1,0:T(8,128)S(1)} %get-tuple-element.520), channel_id=1, source_target_pairs={{1,0},{2,1},{3,2},{4,3},{5,4},{6,5},{7,6},{9,8},{10,9},{11,10},{12... | collective-permute-start | bytes 1572872 | tf_op jit(solution)/shard_map/while/body/eval_jaxpr/ppermute | solution.py:19
  586.7 14.2 %all-to-all-start.2 = ((f32[512,1,256]{2,1,0:T(1,128)}), f32[512,1,256]{2,1,0:T(1,128)S(1)}, u32[]{:S(2)}, u32[]{:S(2)}) async-start(f32[512,1,256]{2,1,0:T(1,128)} %copy.136), calls=%async_computation.2 | async-start | bytes 1048576 | tf_op jit(solution)/shard_map/while/body/eval_jaxpr/all_to_all | solution.py:141
  605.9 16.8 %collective-permute-start = (f32[32,4096]{1,0:T(8,128)S(1)}, f32[32,4096]{1,0:T(8,128)S(1)}, u32[]{:S(2)}, u32[]{:S(2)}) collective-permute-start(f32[32,4096]{1,0:T(8,128)S(1)} %get-tuple-element.520), channel_id=1, source_target_pairs={{1,0},{2,1},{3,2},{4,3},{5,4},{6,5},{7,6},{9,8},{10,9},{11,10},{12... | collective-permute-start | bytes 1572872 | tf_op jit(solution)/shard_map/while/body/eval_jaxpr/ppermute | solution.py:19
  668.4 14.2 %all-to-all-start.2 = ((f32[512,1,256]{2,1,0:T(1,128)}), f32[512,1,256]{2,1,0:T(1,128)S(1)}, u32[]{:S(2)}, u32[]{:S(2)}) async-start(f32[512,1,256]{2,1,0:T(1,128)} %copy.136), calls=%async_computation.2 | async-start | bytes 1048576 | tf_op jit(solution)/shard_map/while/body/eval_jaxpr/all_to_all | solution.py:141
  687.5 16.8 %collective-permute-start = (f32[32,4096]{1,0:T(8,128)S(1)}, f32[32,4096]{1,0:T(8,128)S(1)}, u32[]{:S(2)}, u32[]{:S(2)}) collective-permute-start(f32[32,4096]{1,0:T(8,128)S(1)} %get-tuple-element.520), channel_id=1, source_target_pairs={{1,0},{2,1},{3,2},{4,3},{5,4},{6,5},{7,6},{9,8},{10,9},{11,10},{12... | collective-permute-start | bytes 1572872 | tf_op jit(solution)/shard_map/while/body/eval_jaxpr/ppermute | solution.py:19
  750.0 14.2 %all-to-all-start.2 = ((f32[512,1,256]{2,1,0:T(1,128)}), f32[512,1,256]{2,1,0:T(1,128)S(1)}, u32[]{:S(2)}, u32[]{:S(2)}) async-start(f32[512,1,256]{2,1,0:T(1,128)} %copy.136), calls=%async_computation.2 | async-start | bytes 1048576 | tf_op jit(solution)/shard_map/while/body/eval_jaxpr/all_to_all | solution.py:141
  769.2 16.8 %collective-permute-start = (f32[32,4096]{1,0:T(8,128)S(1)}, f32[32,4096]{1,0:T(8,128)S(1)}, u32[]{:S(2)}, u32[]{:S(2)}) collective-permute-start(f32[32,4096]{1,0:T(8,128)S(1)} %get-tuple-element.520), channel_id=1, source_target_pairs={{1,0},{2,1},{3,2},{4,3},{5,4},{6,5},{7,6},{9,8},{10,9},{11,10},{12... | collective-permute-start | bytes 1572872 | tf_op jit(solution)/shard_map/while/body/eval_jaxpr/ppermute | solution.py:19
  831.7 14.2 %all-to-all-start.2 = ((f32[512,1,256]{2,1,0:T(1,128)}), f32[512,1,256]{2,1,0:T(1,128)S(1)}, u32[]{:S(2)}, u32[]{:S(2)}) async-start(f32[512,1,256]{2,1,0:T(1,128)} %copy.136), calls=%async_computation.2 | async-start | bytes 1048576 | tf_op jit(solution)/shard_map/while/body/eval_jaxpr/all_to_all | solution.py:141
  850.9 16.8 %collective-permute-start = (f32[32,4096]{1,0:T(8,128)S(1)}, f32[32,4096]{1,0:T(8,128)S(1)}, u32[]{:S(2)}, u32[]{:S(2)}) collective-permute-start(f32[32,4096]{1,0:T(8,128)S(1)} %get-tuple-element.520), channel_id=1, source_target_pairs={{1,0},{2,1},{3,2},{4,3},{5,4},{6,5},{7,6},{9,8},{10,9},{11,10},{12... | collective-permute-start | bytes 1572872 | tf_op jit(solution)/shard_map/while/body/eval_jaxpr/ppermute | solution.py:19
  913.4 14.2 %all-to-all-start.2 = ((f32[512,1,256]{2,1,0:T(1,128)}), f32[512,1,256]{2,1,0:T(1,128)S(1)}, u32[]{:S(2)}, u32[]{:S(2)}) async-start(f32[512,1,256]{2,1,0:T(1,128)} %copy.136), calls=%async_computation.2 | async-start | bytes 1048576 | tf_op jit(solution)/shard_map/while/body/eval_jaxpr/all_to_all | solution.py:141
  932.5 16.8 %collective-permute-start = (f32[32,4096]{1,0:T(8,128)S(1)}, f32[32,4096]{1,0:T(8,128)S(1)}, u32[]{:S(2)}, u32[]{:S(2)}) collective-permute-start(f32[32,4096]{1,0:T(8,128)S(1)} %get-tuple-element.520), channel_id=1, source_target_pairs={{1,0},{2,1},{3,2},{4,3},{5,4},{6,5},{7,6},{9,8},{10,9},{11,10},{12... | collective-permute-start | bytes 1572872 | tf_op jit(solution)/shard_map/while/body/eval_jaxpr/ppermute | solution.py:19
  995.0 14.2 %all-to-all-start.2 = ((f32[512,1,256]{2,1,0:T(1,128)}), f32[512,1,256]{2,1,0:T(1,128)S(1)}, u32[]{:S(2)}, u32[]{:S(2)}) async-start(f32[512,1,256]{2,1,0:T(1,128)} %copy.136), calls=%async_computation.2 | async-start | bytes 1048576 | tf_op jit(solution)/shard_map/while/body/eval_jaxpr/all_to_all | solution.py:141
  1014.2 16.8 %collective-permute-start = (f32[32,4096]{1,0:T(8,128)S(1)}, f32[32,4096]{1,0:T(8,128)S(1)}, u32[]{:S(2)}, u32[]{:S(2)}) collective-permute-start(f32[32,4096]{1,0:T(8,128)S(1)} %get-tuple-element.520), channel_id=1, source_target_pairs={{1,0},{2,1},{3,2},{4,3},{5,4},{6,5},{7,6},{9,8},{10,9},{11,10},{12... | collective-permute-start | bytes 1572872 | tf_op jit(solution)/shard_map/while/body/eval_jaxpr/ppermute | solution.py:19
  1064.3 144.8 %reduce-scatter.9.cloned.1.call-start = ((), (), s32[]{:S(2)}) async-start(), calls=%async_computation.12 | async-start | bytes 1179648
  (165 other events, 1226.6 us)
Sparse Core Ops, SparseCore 0:
  10.3 48.4 all-gather.4
  61.1 46.6 all-gather.2
  1064.4 70.0 reduce-scatter.6
  1138.4 70.6 reduce-scatter.8
where the time goes:
time: 1220 us
  waiting for transfers between devices  547 us (45%)
  starting transfers between devices  178 us (15%)
  matrix products  150 us (12%)
  other arithmetic  148 us (12%)
  local copies, waits for them, and re-layouts  137 us (11%)
  blocking collectives  40.2 us (3%)
  between operations  13.9 us (1%)
    unnamed x6, waiting for transfers between devices  118 us
    ppermute x11, waiting for transfers between devices, passed_along(): lax.ppermute(value, axis, [(source, source + steps) for source in range(f...  115 us
    all_to_all x11, waiting for transfers between devices, one_turn(): lax.all_to_all(query_grad.reshape(ctx_count * block_rows, 1, local_width)...  109 us
    sub x11, matrix products, attend_block(): probs = jnp.exp(scores - row_max)  71.1 us
    while x341, local copies, waits for them, and re-layouts  62.1 us
    all_to_all x11, waiting for transfers between devices, one_turn(): lax.all_to_all(outgoing[0], 'ctx', split_axis=1, concat_axis=0, tiled=True)  58 us
    all_to_all x11, starting transfers between devices, one_turn(): lax.all_to_all(outgoing[1], 'ctx', split_axis=1, concat_axis=0, tiled=True)  55.9 us
    convert_element_type x11, other arithmetic, attend_block(): probs_low = probs.astype(jnp.bfloat16)  52.7 us
  transfers between devices with their start and end apart: 50, of which 49 were waited for; matrix products, arithmetic and copies ran while one was open for 8% of the time, Pallas kernels for 0%

commit v1 on v0

v1 whole, which is shorter than its diff:
```python
import functools
import math

import jax
import jax.numpy as jnp
from jax import lax
from jax.experimental import pallas as pl
from jax.experimental.pallas import tpu as pltpu
from jax.sharding import PartitionSpec as P

H = 32
HD = 128
LAYERS = 8
N_CTX = 16
TOK_DEV = 128
HEADS_SEC = 4
QUARTERS = 4
ROWS = TOK_DEV // QUARTERS
NQ = N_CTX * ROWS
NK = N_CTX * TOK_DEV
CHUNKS = 4
CK = NK // CHUNKS
CQ = NQ // CHUNKS

masked_score = -1e30
norm_eps = 1e-06
factor = 1.0 / math.sqrt(HD)
log2e = math.log2(math.e)

NT = (((1,), (1,)), ((), ()))
NN = (((1,), (0,)), ((), ()))


def dot(a, b, dims):
    return lax.dot_general(a, b, dims, preferred_element_type=jnp.float32)


def attend_kernel(
    place_ref,
    block_ref,
    x_ref,
    gain_ref,
    k_in,
    v_in,
    top_ref,
    g_out,
    dk_out,
    dv_out,
    k_ref,
    v_ref,
    kt_ref,
    s_ref,
    dp_ref,
    g_ref,
    dk_ref,
    dv_ref,
):
    quarter = lax.axis_index("ctx") % QUARTERS
    for p in range(N_CTX):
        b = block_ref[p]
        k_ref[p * TOK_DEV : (p + 1) * TOK_DEV, :] = k_in[b]
        v_ref[p * TOK_DEV : (p + 1) * TOK_DEV, :] = v_in[b]
        g_ref[p * ROWS : (p + 1) * ROWS, :] = top_ref[b].astype(jnp.float32)
    for j in range(CHUNKS):
        rows = slice(j * CK, (j + 1) * CK)
        kt_ref[:, rows] = jnp.transpose(k_ref[rows, :])
    dk_ref[...] = jnp.zeros_like(dk_ref)
    dv_ref[...] = jnp.zeros_like(dv_ref)

    lane = lax.broadcasted_iota(jnp.int32, (1, CQ), 1)
    query_at = (lane // ROWS) * TOK_DEV + quarter * ROWS + lane % ROWS
    key_at = lax.broadcasted_iota(jnp.int32, (CK, CQ), 0)
    seen = key_at <= query_at

    def one_layer(step, carry):
        layer = LAYERS - 1 - step
        xf = jnp.concatenate(
            [x_ref[block_ref[p], layer] for p in range(N_CTX)], axis=0
        ).astype(jnp.float32)
        gain = gain_ref[pl.ds(layer, 1), :]
        inv_rms = lax.rsqrt(jnp.mean(xf * xf, axis=1, keepdims=True) + norm_eps)
        query = (xf * inv_rms * gain).astype(jnp.bfloat16)
        grad = g_ref[...].astype(jnp.bfloat16)

        tops = []
        for j in range(CHUNKS):
            rows, first = slice(j * CK, (j + 1) * CK), j * CQ
            s = dot(k_ref[rows, :], query[first:, :], NT)
            diag = jnp.where(seen, s[:, :CQ], masked_score)
            s_ref[rows, first : first + CQ] = diag
            top = jnp.max(diag, axis=0, keepdims=True)
            if j < CHUNKS - 1:
                s_ref[rows, first + CQ :] = s[:, CQ:]
                top = jnp.concatenate([top, jnp.max(s[:, CQ:], axis=0, keepdims=True)], axis=1)
            tops.append(top)
        row_max = tops[0]
        for j in range(1, CHUNKS):
            row_max = jnp.concatenate(
                [row_max[:, : j * CQ], jnp.maximum(row_max[:, j * CQ :], tops[j])], axis=1
            )

        def add_from(total, part, first):
            if first == 0:
                return part if total is None else total + part
            return jnp.concatenate([total[:, :first], total[:, first:] + part], axis=1)

        total = None
        for j in range(CHUNKS):
            rows, first = slice(j * CK, (j + 1) * CK), j * CQ
            e = jnp.exp2((s_ref[rows, first:] - row_max[:, first:]) * (factor * log2e))
            s_ref[rows, first:] = e
            total = add_from(total, jnp.sum(e, axis=0, keepdims=True), first)
        inv_total = 1.0 / total

        delta = None
        for j in range(CHUNKS):
            rows, first = slice(j * CK, (j + 1) * CK), j * CQ
            dp = dot(v_ref[rows, :], grad[first:, :], NT)
            dp_ref[rows, first:] = dp
            probs = s_ref[rows, first:] * inv_total[:, first:]
            s_ref[rows, first:] = probs
            low = probs.astype(jnp.bfloat16)
            delta = add_from(
                delta, jnp.sum(low.astype(jnp.float32) * dp, axis=0, keepdims=True), first
            )
            dv_ref[rows, :] += dot(low, grad[first:, :], NN)

        dq_t = None
        for j in range(CHUNKS):
            rows, first = slice(j * CK, (j + 1) * CK), j * CQ
            ds = (s_ref[rows, first:] * (dp_ref[rows, first:] - delta[:, first:])).astype(
                jnp.bfloat16
            )
            dk_ref[rows, :] += dot(ds, query[first:, :], NN)
            dq_t = add_from(dq_t, dot(kt_ref[:, rows], ds, NN), first)
        scaled = jnp.transpose(dq_t) * (gain * factor)
        inner = jnp.mean(scaled * xf, axis=1, keepdims=True)
        g_ref[...] += inv_rms * scaled - xf * (inv_rms * inv_rms * inv_rms) * inner
        for b in range(N_CTX):
            at = pl.ds(pl.multiple_of(place_ref[b] * ROWS, ROWS), ROWS)
            g_out[b, pl.ds(layer, 1)] = g_ref[at, :].astype(jnp.bfloat16)[None]
        return carry

    lax.fori_loop(0, LAYERS, one_layer, 0)
    for b in range(N_CTX):
        at = pl.ds(pl.multiple_of(place_ref[b] * TOK_DEV, TOK_DEV), TOK_DEV)
        dk_out[b] = (dk_ref[at, :] * factor).astype(jnp.bfloat16)
        dv_out[b] = dv_ref[at, :].astype(jnp.bfloat16)


def attend(places, blocks, x, gains, keys, values, top):
    smem = pl.BlockSpec(memory_space=pltpu.SMEM)
    vmem = pl.BlockSpec(memory_space=pltpu.VMEM)
    return pl.pallas_call(
        attend_kernel,
        out_shape=(
            jax.ShapeDtypeStruct((N_CTX, LAYERS, ROWS, HD), jnp.bfloat16),
            jax.ShapeDtypeStruct((N_CTX, TOK_DEV, HD), jnp.bfloat16),
            jax.ShapeDtypeStruct((N_CTX, TOK_DEV, HD), jnp.bfloat16),
        ),
        in_specs=[smem, smem, vmem, vmem, vmem, vmem, vmem],
        out_specs=(vmem, vmem, vmem),
        scratch_shapes=[
            pltpu.VMEM((NK, HD), jnp.bfloat16),
            pltpu.VMEM((NK, HD), jnp.bfloat16),
            pltpu.VMEM((HD, NK), jnp.bfloat16),
            pltpu.VMEM((NK, NQ), jnp.float32),
            pltpu.VMEM((NK, NQ), jnp.float32),
            pltpu.VMEM((NQ, HD), jnp.float32),
            pltpu.VMEM((NK, HD), jnp.float32),
            pltpu.VMEM((NK, HD), jnp.float32),
        ],
        compiler_params=pltpu.CompilerParams(vmem_limit_bytes=56 * 2**20),
    )(places, blocks, x, gains, keys, values, top)


def swap(value, axis):
    return lax.all_to_all(value, axis, split_axis=0, concat_axis=0, tiled=True)


def body(x_saved, gains, keys, values, grad_top, block_order):
    section = lax.axis_index("section")
    head = lax.axis_index("ctx") // QUARTERS
    wide = HEADS_SEC * HD
    n_sec = lax.axis_size("section")
    blocks = jnp.sum(
        jnp.where(
            block_order[None, :] == jnp.arange(N_CTX, dtype=jnp.int32)[:, None],
            jnp.arange(N_CTX, dtype=jnp.int32)[None, :],
            0,
        ),
        axis=1,
        dtype=jnp.int32,
    )

    x = swap(x_saved[0].reshape(TOK_DEV, n_sec, wide).transpose(1, 0, 2), "section")
    x = x.reshape(LAYERS, QUARTERS, ROWS, HEADS_SEC, HD).transpose(3, 1, 0, 2, 4)
    x = swap(x.reshape(N_CTX, LAYERS, ROWS, HD), "ctx")

    def spread(value):
        value = swap(value.reshape(-1, n_sec, wide).transpose(1, 0, 2), "section")
        value = value.reshape(TOK_DEV, HEADS_SEC, 1, HD).transpose(1, 2, 0, 3)
        value = jnp.broadcast_to(value, (HEADS_SEC, QUARTERS, TOK_DEV, HD))
        return swap(value.reshape(N_CTX, TOK_DEV, HD), "ctx")

    k, v = spread(keys), spread(values)
    gain = swap(gains.reshape(n_sec, wide), "section")
    gain = lax.dynamic_slice_in_dim(gain, head * HD, HD, 1)
    top = lax.dynamic_slice_in_dim(grad_top, section * wide, wide, 1)
    top = top.reshape(QUARTERS, ROWS, HEADS_SEC, HD).transpose(2, 0, 1, 3)
    top = swap(top.reshape(N_CTX, ROWS, HD), "ctx")

    g, dk, dv = attend(block_order, blocks, x, gain, k, v, top)

    g = swap(g, "ctx").reshape(HEADS_SEC, QUARTERS, LAYERS, ROWS, HD).transpose(2, 1, 3, 0, 4)
    g = swap(g.reshape(LAYERS, TOK_DEV, wide), "section")
    g = g.transpose(1, 0, 2).reshape(1, TOK_DEV, H * HD).astype(jnp.float32)

    def gather(value):
        value = swap(value, "ctx").reshape(HEADS_SEC, QUARTERS, TOK_DEV, HD)
        value = jnp.sum(value.astype(jnp.float32), axis=1).astype(jnp.bfloat16)
        value = value.transpose(1, 0, 2).reshape(n_sec, TOK_DEV // n_sec, wide)
        value = swap(value, "section")
        return value.transpose(1, 0, 2).reshape(-1, H * HD).astype(jnp.float32)

    return (g, gather(dk), gather(dv))


def solution(mesh):
    placed = (
        P("section", "ctx", None),
        P("section", None),
        P(("ctx", "section"), None),
        P(("ctx", "section"), None),
        P("ctx", None),
        P(),
    )
    return jax.shard_map(
        body,
        mesh=mesh,
        in_specs=placed,
        out_specs=(
            P("section", "ctx", None),
            P(("ctx", "section"), None),
            P(("ctx", "section"), None),
        ),
        check_vma=False,
    )
```

time: 1220 us -> 250 us (0.20)
  waiting for transfers between devices: 547 us -> 113 us
  matrix products: 150 us -> 0 us
  other arithmetic: 148 us -> 2.32 us
  starting transfers between devices: 178 us -> 60.6 us
  local copies, waits for them, and re-layouts: 137 us -> 20.5 us
  Pallas kernels: 0 us -> 26.3 us
  blocking collectives: 40.2 us -> 23.5 us
  between operations: 13.9 us -> 0.83 us
    unnamed x6 -> x0, waiting for transfers between devices: 118 us -> none
    ppermute x11 -> x0, waiting for transfers between devices: 115 us -> none  [passed_along(): lax.ppermute(value, axis, [(source, source + steps) for source in range(f...]
    all_to_all x35 -> x12, waiting for transfers between devices: 223 us -> 113 us  [swap(): return lax.all_to_all(value, axis, split_axis=0, concat_axis=0, tiled=True)]
    all_to_all x35 -> x12, starting transfers between devices: 164 us -> 60.6 us  [swap(): return lax.all_to_all(value, axis, split_axis=0, concat_axis=0, tiled=True)]
    all_gather x2 -> x0, waiting for transfers between devices: 90.7 us -> none  [the longest x1 50.1 us: body(): lax.all_gather(values, 'section', axis=0, tiled=True)]
    dot_general x55 -> x0, matrix products: 78.6 us -> none  [the longest x11 18.8 us: attend_block(): jnp.einsum('qhd,khd->hqk', grad_heads, values_heads, preferred_element_ty...]
    convert_element_type x38 -> x1, other arithmetic: 73.5 us -> 1.5 us  [body(): g = g.transpose(1, 0, 2).reshape(1, TOK_DEV, H * HD).astype(jnp.float32)]
    sub x11 -> x0, matrix products: 71.1 us -> none  [attend_block(): probs = jnp.exp(scores - row_max)]
  transfers between devices with their start and end apart: 50 -> 12, of which waited for: 49 -> 12; matrix products, arithmetic and copies ran while one was open for 8% -> 5% of each run, Pallas kernels for 0% -> 0%
where the time goes in v1:
time: 250 us; the launch traced here: 247 us
  waiting for transfers between devices  113 us (45%)
  starting transfers between devices  60.6 us (24%)
  Pallas kernels  26.3 us (11%)
  blocking collectives  23.5 us (9%)
  local copies, waits for them, and re-layouts  20.5 us (8%)
    all_to_all x12, waiting for transfers between devices, swap(): return lax.all_to_all(value, axis, split_axis=0, concat_axis=0, tiled=True)  113 us
    all_to_all x12, starting transfers between devices, swap(): return lax.all_to_all(value, axis, split_axis=0, concat_axis=0, tiled=True)  60.6 us
    pallas_call x1, Pallas kernels, attend(): pl.pallas_call(attend_kernel, out_shape=(jax.ShapeDtypeStruct((N_CTX, LAY...  26.3 us
    all_to_all x2, blocking collectives, swap(): return lax.all_to_all(value, axis, split_axis=0, concat_axis=0, tiled=True)  23.5 us
    unnamed x14, local copies, waits for them, and re-layouts  5.06 us
  transfers between devices with their start and end apart: 12, of which 12 were waited for; matrix products, arithmetic and copies ran while one was open for 5% of the time, Pallas kernels for 0%

profile of v1, /device:TPU:1, one launch (start us, length us, event | category | flops | bytes accessed | tf_op | source)
XLA Modules:
  0.0 247.0 jit_solution(17740861231226783450)
XLA Ops:
  0.6 8.5 %all-to-all-start.2 = ((f32[8,1,512]{2,1,0:T(1,128)}), f32[8,1,512]{2,1,0:T(1,128)S(1)}, u32[]{:S(2)}, u32[]{:S(2)}) async-start(f32[8,1,512]{2,1,0:T(1,128)} %bitcast.71), calls=%async_computation.2 | async-start | bytes 32768 | tf_op jit(solution)/shard_map/all_to_all | solution.py:178
  9.1 1.6 copy.69
  10.7 5.0 %all-to-all-done.2 = f32[8,1,512]{2,1,0:T(1,128)S(1)} async-done(((f32[8,1,512]{2,1,0:T(1,128)}), f32[8,1,512]{2,1,0:T(1,128)S(1)}, u32[]{:S(2)}, u32[]{:S(2)}) %all-to-all-start.2) | async-done | bytes 16416 | tf_op jit(solution)/shard_map/all_to_all | solution.py:178
  15.7 3.4 %all-to-all-start.3 = ((bf16[8,16,512]{2,1,0:T(8,128)(2,1)}), bf16[8,16,512]{2,1,0:T(8,128)(2,1)S(1)}, u32[]{:S(2)}, u32[]{:S(2)}) async-start(bf16[8,16,512]{2,1,0:T(8,128)(2,1)} %bitcast.54), calls=%async_computation.3 | async-start | bytes 262144 | tf_op jit(solution)/shard_map/all_to_all | solution.py:178
  19.1 1.6 copy.68
  20.6 5.5 %all-to-all-done.3 = bf16[8,16,512]{2,1,0:T(8,128)(2,1)S(1)} async-done(((bf16[8,16,512]{2,1,0:T(8,128)(2,1)}), bf16[8,16,512]{2,1,0:T(8,128)(2,1)S(1)}, u32[]{:S(2)}, u32[]{:S(2)}) %all-to-all-start.3) | async-done | bytes 131104 | tf_op jit(solution)/shard_map/all_to_all | solution.py:178
  26.1 3.4 %all-to-all-start.5 = ((bf16[8,16,512]{2,1,0:T(8,128)(2,1)}), bf16[8,16,512]{2,1,0:T(8,128)(2,1)S(1)}, u32[]{:S(2)}, u32[]{:S(2)}) async-start(bf16[8,16,512]{2,1,0:T(8,128)(2,1)} %bitcast.52), calls=%async_computation.5 | async-start | bytes 262144 | tf_op jit(solution)/shard_map/all_to_all | solution.py:178
  30.2 6.2 %all-to-all-done.5 = bf16[8,16,512]{2,1,0:T(8,128)(2,1)S(1)} async-done(((bf16[8,16,512]{2,1,0:T(8,128)(2,1)}), bf16[8,16,512]{2,1,0:T(8,128)(2,1)S(1)}, u32[]{:S(2)}, u32[]{:S(2)}) %all-to-all-start.5) | async-done | bytes 131104 | tf_op jit(solution)/shard_map/all_to_all | solution.py:178
  36.5 8.9 %all-to-all-start.7 = ((bf16[16,32,128]{2,1,0:T(8,128)(2,1)}), bf16[16,32,128]{2,1,0:T(8,128)(2,1)S(1)}, u32[]{:S(2)}, u32[]{:S(2)}) async-start(bf16[16,32,128]{2,1,0:T(8,128)(2,1)} %bitcast.14), calls=%async_computation.7 | async-start | bytes 262144 | tf_op jit(solution)/shard_map/all_to_all | solution.py:178
  45.4 6.1 %all-to-all-done.7.top_ref = bf16[16,32,128]{2,1,0:T(8,128)(2,1)S(1)} async-done(((bf16[16,32,128]{2,1,0:T(8,128)(2,1)}), bf16[16,32,128]{2,1,0:T(8,128)(2,1)S(1)}, u32[]{:S(2)}, u32[]{:S(2)}) %all-to-all-start.7) | async-done | bytes 131104 | tf_op jit(solution)/shard_map/all_to_all | solution.py:178
  52.4 4.0 %all-to-all-start.6 = ((bf16[16,128,128]{2,1,0:T(8,128)(2,1)}), bf16[16,128,128]{2,1,0:T(8,128)(2,1)S(1)}, u32[]{:S(2)}, u32[]{:S(2)}) async-start(bf16[16,128,128]{2,1,0:T(8,128)(2,1)} %bitcast.12), calls=%async_computation.6 | async-start | bytes 1048576 | tf_op jit(solution)/shard_map/all_to_all | solution.py:178
  58.1 8.2 %all-to-all-done.6.v_in = bf16[16,128,128]{2,1,0:T(8,128)(2,1)S(1)} async-done(((bf16[16,128,128]{2,1,0:T(8,128)(2,1)}), bf16[16,128,128]{2,1,0:T(8,128)(2,1)S(1)}, u32[]{:S(2)}, u32[]{:S(2)}) %all-to-all-start.6) | async-done | bytes 524320 | tf_op jit(solution)/shard_map/all_to_all | solution.py:178
  67.1 3.6 %all-to-all-start = ((bf16[8,128,512]{2,1,0:T(8,128)(2,1)}), bf16[8,128,512]{2,1,0:T(8,128)(2,1)S(1)}, u32[]{:S(2)}, u32[]{:S(2)}) async-start(bf16[8,128,512]{2,1,0:T(8,128)(2,1)} %bitcast.50), calls=%async_computation | async-start | bytes 2097152 | tf_op jit(solution)/shard_map/all_to_all | solution.py:178
  70.7 15.6 %all-to-all-done = bf16[8,128,512]{2,1,0:T(8,128)(2,1)S(1)} async-done(((bf16[8,128,512]{2,1,0:T(8,128)(2,1)}), bf16[8,128,512]{2,1,0:T(8,128)(2,1)S(1)}, u32[]{:S(2)}, u32[]{:S(2)}) %all-to-all-start) | async-done | bytes 1048608 | tf_op jit(solution)/shard_map/all_to_all | solution.py:178
  87.3 6.4 %all-to-all-start.4 = ((bf16[16,128,128]{2,1,0:T(8,128)(2,1)}), bf16[16,128,128]{2,1,0:T(8,128)(2,1)}, u32[]{:S(2)}, u32[]{:S(2)}) async-start(bf16[16,128,128]{2,1,0:T(8,128)(2,1)} %bitcast.8), calls=%async_computation.4 | async-start | bytes 1048576 | tf_op jit(solution)/shard_map/all_to_all | solution.py:178
  95.1 8.5 %all-to-all-done.4.k_in = bf16[16,128,128]{2,1,0:T(8,128)(2,1)} async-done(((bf16[16,128,128]{2,1,0:T(8,128)(2,1)}), bf16[16,128,128]{2,1,0:T(8,128)(2,1)}, u32[]{:S(2)}, u32[]{:S(2)}) %all-to-all-start.4) | async-done | bytes 524320 | tf_op jit(solution)/shard_map/all_to_all | solution.py:178
  103.6 4.6 %all-to-all-start.1 = ((bf16[16,8,32,128]{3,2,1,0:T(8,128)(2,1)}), bf16[16,8,32,128]{3,2,1,0:T(8,128)(2,1)S(1)}, u32[]{:S(2)}, u32[]{:S(2)}) async-start(bf16[16,8,32,128]{3,2,1,0:T(8,128)(2,1)} %bitcast.2), calls=%async_computation.1 | async-start | bytes 2097152 | tf_op jit(solution)/shard_map/all_to_all | solution.py:178
  109.5 14.7 %all-to-all-done.1.x_ref = bf16[16,8,32,128]{3,2,1,0:T(8,128)(2,1)S(1)} async-done(((bf16[16,8,32,128]{3,2,1,0:T(8,128)(2,1)}), bf16[16,8,32,128]{3,2,1,0:T(8,128)(2,1)S(1)}, u32[]{:S(2)}, u32[]{:S(2)}) %all-to-all-start.1) | async-done | bytes 1048608 | tf_op jit(solution)/shard_map/all_to_all | solution.py:178
  125.1 26.3 %shard_map.85 = (bf16[16,8,32,128]{3,2,1,0:T(8,128)(2,1)}, bf16[16,128,128]{2,1,0:T(8,128)(2,1)}, bf16[16,128,128]{2,1,0:T(8,128)(2,1)}) custom-call(s32[16]{0:T(128)} %place_ref.1, s32[16]{0:T(128)} %select_reduce_fusion.block_ref, bf16[16,8,32,128]{3,2,1,0:T(8,128)(2,1)} %copy-done.1, f32[8,128]{1,0:T(8,128)} %bitcast.70, ...), custom_call_target="tpu_custom_call" | custom-call | tf_op jit(solution)/shard_map/pallas_call | solution.py:154
  151.4 14.1 %all_to_all.74 = bf16[16,128,128]{2,1,0:T(8,128)(2,1)S(1)} all-to-all(bf16[16,128,128]{2,1,0:T(8,128)(2,1)} %get-tuple-element.7), channel_id=1, replica_groups=mesh['ctx'=16,'section'=8] {'ctx'}, dimensions={0} | all-to-all | bytes 1048576 | tf_op jit(solution)/shard_map/all_to_all | solution.py:178
  165.5 4.5 %all-to-all-start.12 = ((bf16[16,128,128]{2,1,0:T(8,128)(2,1)}), bf16[16,128,128]{2,1,0:T(8,128)(2,1)S(1)}, u32[]{:S(2)}, u32[]{:S(2)}) async-start(bf16[16,128,128]{2,1,0:T(8,128)(2,1)} %get-tuple-element.8), calls=%async_computation.12 | async-start | bytes 1048576 | tf_op jit(solution)/shard_map/all_to_all | solution.py:178
  170.3 9.6 %all-to-all-done.12 = bf16[16,128,128]{2,1,0:T(8,128)(2,1)S(1)} async-done(((bf16[16,128,128]{2,1,0:T(8,128)(2,1)}), bf16[16,128,128]{2,1,0:T(8,128)(2,1)S(1)}, u32[]{:S(2)}, u32[]{:S(2)}) %all-to-all-start.12) | async-done | bytes 524320 | tf_op jit(solution)/shard_map/all_to_all | solution.py:178
  179.9 9.4 %all_to_all.75 = bf16[8,16,512]{2,1,0:T(8,128)(2,1)S(1)} all-to-all(bf16[8,16,512]{2,1,0:T(8,128)(2,1)S(1)} %reshape.94), channel_id=1, replica_groups=mesh['ctx'=16,'section'=8] {'section'}, dimensions={0} | all-to-all | bytes 262144 | tf_op jit(solution)/shard_map/all_to_all | solution.py:178
  189.4 5.9 %all-to-all-start.8 = ((bf16[16,8,32,128]{3,2,1,0:T(8,128)(2,1)}), bf16[16,8,32,128]{3,2,1,0:T(8,128)(2,1)S(1)}, u32[]{:S(2)}, u32[]{:S(2)}) async-start(bf16[16,8,32,128]{3,2,1,0:T(8,128)(2,1)} %get-tuple-element.6), calls=%async_computation.8 | async-start | bytes 2097152 | tf_op jit(solution)/shard_map/all_to_all | solution.py:178
  196.1 15.0 %all-to-all-done.8 = bf16[16,8,32,128]{3,2,1,0:T(8,128)(2,1)S(1)} async-done(((bf16[16,8,32,128]{3,2,1,0:T(8,128)(2,1)}), bf16[16,8,32,128]{3,2,1,0:T(8,128)(2,1)S(1)}, u32[]{:S(2)}, u32[]{:S(2)}) %all-to-all-start.8) | async-done | bytes 1048608 | tf_op jit(solution)/shard_map/all_to_all | solution.py:178
  211.2 3.4 %all-to-all-start.13 = ((bf16[8,16,512]{2,1,0:T(8,128)(2,1)}), bf16[8,16,512]{2,1,0:T(8,128)(2,1)S(1)}, u32[]{:S(2)}, u32[]{:S(2)}) async-start(bf16[8,16,512]{2,1,0:T(8,128)(2,1)} %reshape.96), calls=%async_computation.13 | async-start | bytes 262144 | tf_op jit(solution)/shard_map/all_to_all | solution.py:178
  216.6 4.9 %all-to-all-done.13 = bf16[8,16,512]{2,1,0:T(8,128)(2,1)S(1)} async-done(((bf16[8,16,512]{2,1,0:T(8,128)(2,1)}), bf16[8,16,512]{2,1,0:T(8,128)(2,1)S(1)}, u32[]{:S(2)}, u32[]{:S(2)}) %all-to-all-start.13) | async-done | bytes 131104 | tf_op jit(solution)/shard_map/all_to_all | solution.py:178
  221.5 4.2 %all-to-all-start.9 = ((bf16[8,128,512]{2,1,0:T(8,128)(2,1)}), bf16[8,128,512]{2,1,0:T(8,128)(2,1)}, u32[]{:S(2)}, u32[]{:S(2)}) async-start(bf16[8,128,512]{2,1,0:T(8,128)(2,1)} %reshape.92), calls=%async_computation.9 | async-start | bytes 2097152 | tf_op jit(solution)/shard_map/all_to_all | solution.py:178
  227.3 13.5 %all-to-all-done.9 = bf16[8,128,512]{2,1,0:T(8,128)(2,1)} async-done(((bf16[8,128,512]{2,1,0:T(8,128)(2,1)}), bf16[8,128,512]{2,1,0:T(8,128)(2,1)}, u32[]{:S(2)}, u32[]{:S(2)}) %all-to-all-start.9) | async-done | bytes 1048608 | tf_op jit(solution)/shard_map/all_to_all | solution.py:178
  240.8 1.5 convert_bitcast_fusion
  242.3 1.8 copy.51
  244.1 2.9 %copy.56 = f32[1,128,4096]{2,1,0:T(8,128)} copy(f32[1,128,4096]{1,2,0:T(8,128)} %bitcast.55) | data formatting | bytes 4194304
  (39 shorter events, 13.4 us)
Async XLA Ops:
  0.6 28.9 %copy-start = (bf16[128,4096]{1,0:T(8,128)(2,1)S(1)}, bf16[128,4096]{1,0:T(8,128)(2,1)}, u32[]{:S(2)}) copy-start(bf16[128,4096]{1,0:T(8,128)(2,1)} %param.10) | copy-start | bytes 3145732
  0.6 15.0 %all-to-all-start.2 = ((f32[8,1,512]{2,1,0:T(1,128)}), f32[8,1,512]{2,1,0:T(1,128)S(1)}, u32[]{:S(2)}, u32[]{:S(2)}) async-start(f32[8,1,512]{2,1,0:T(1,128)} %bitcast.71), calls=%async_computation.2 | async-start | bytes 32768 | tf_op jit(solution)/shard_map/all_to_all | solution.py:178
  10.7 45.7 %copy-start.3 = (bf16[1,128,4096]{2,1,0:T(8,128)(2,1)S(1)}, bf16[1,128,4096]{2,1,0:T(8,128)(2,1)}, u32[]{:S(2)}) copy-start(bf16[1,128,4096]{2,1,0:T(8,128)(2,1)} %param.6) | copy-start | bytes 3145732
  15.7 10.4 %all-to-all-start.3 = ((bf16[8,16,512]{2,1,0:T(8,128)(2,1)}), bf16[8,16,512]{2,1,0:T(8,128)(2,1)S(1)}, u32[]{:S(2)}, u32[]{:S(2)}) async-start(bf16[8,16,512]{2,1,0:T(8,128)(2,1)} %bitcast.54), calls=%async_computation.3 | async-start | bytes 262144 | tf_op jit(solution)/shard_map/all_to_all | solution.py:178
  26.1 10.4 %all-to-all-start.5 = ((bf16[8,16,512]{2,1,0:T(8,128)(2,1)}), bf16[8,16,512]{2,1,0:T(8,128)(2,1)S(1)}, u32[]{:S(2)}, u32[]{:S(2)}) async-start(bf16[8,16,512]{2,1,0:T(8,128)(2,1)} %bitcast.52), calls=%async_computation.5 | async-start | bytes 262144 | tf_op jit(solution)/shard_map/all_to_all | solution.py:178
  36.5 15.0 %all-to-all-start.7 = ((bf16[16,32,128]{2,1,0:T(8,128)(2,1)}), bf16[16,32,128]{2,1,0:T(8,128)(2,1)S(1)}, u32[]{:S(2)}, u32[]{:S(2)}) async-start(bf16[16,32,128]{2,1,0:T(8,128)(2,1)} %bitcast.14), calls=%async_computation.7 | async-start | bytes 262144 | tf_op jit(solution)/shard_map/all_to_all | solution.py:178
  51.5 6.6 %copy-start.4 = (bf16[16,32,128]{2,1,0:T(8,128)(2,1)}, bf16[16,32,128]{2,1,0:T(8,128)(2,1)S(1)}, u32[]{:S(2)}) copy-start(bf16[16,32,128]{2,1,0:T(8,128)(2,1)S(1)} %all-to-all-done.7.top_ref) | copy-start | bytes 393220
  52.4 13.9 %all-to-all-start.6 = ((bf16[16,128,128]{2,1,0:T(8,128)(2,1)}), bf16[16,128,128]{2,1,0:T(8,128)(2,1)S(1)}, u32[]{:S(2)}, u32[]{:S(2)}) async-start(bf16[16,128,128]{2,1,0:T(8,128)(2,1)} %bitcast.12), calls=%async_computation.6 | async-start | bytes 1048576 | tf_op jit(solution)/shard_map/all_to_all | solution.py:178
  66.3 0.8 copy-start.2
  67.1 19.3 %all-to-all-start = ((bf16[8,128,512]{2,1,0:T(8,128)(2,1)}), bf16[8,128,512]{2,1,0:T(8,128)(2,1)S(1)}, u32[]{:S(2)}, u32[]{:S(2)}) async-start(bf16[8,128,512]{2,1,0:T(8,128)(2,1)} %bitcast.50), calls=%async_computation | async-start | bytes 2097152 | tf_op jit(solution)/shard_map/all_to_all | solution.py:178
  87.3 16.3 %all-to-all-start.4 = ((bf16[16,128,128]{2,1,0:T(8,128)(2,1)}), bf16[16,128,128]{2,1,0:T(8,128)(2,1)}, u32[]{:S(2)}, u32[]{:S(2)}) async-start(bf16[16,128,128]{2,1,0:T(8,128)(2,1)} %bitcast.8), calls=%async_computation.4 | async-start | bytes 1048576 | tf_op jit(solution)/shard_map/all_to_all | solution.py:178
  93.9 14.3 %copy-start.5 = (s32[16]{0:T(128)S(1)}, s32[16]{0:T(128)}, u32[]{:S(2)}) copy-start(s32[16]{0:T(128)} %place_ref.1) | copy-start | bytes 196
  103.6 20.5 %all-to-all-start.1 = ((bf16[16,8,32,128]{3,2,1,0:T(8,128)(2,1)}), bf16[16,8,32,128]{3,2,1,0:T(8,128)(2,1)S(1)}, u32[]{:S(2)}, u32[]{:S(2)}) async-start(bf16[16,8,32,128]{3,2,1,0:T(8,128)(2,1)} %bitcast.2), calls=%async_computation.1 | async-start | bytes 2097152 | tf_op jit(solution)/shard_map/all_to_all | solution.py:178
  124.1 1.0 copy-start.1
  165.5 14.4 %all-to-all-start.12 = ((bf16[16,128,128]{2,1,0:T(8,128)(2,1)}), bf16[16,128,128]{2,1,0:T(8,128)(2,1)S(1)}, u32[]{:S(2)}, u32[]{:S(2)}) async-start(bf16[16,128,128]{2,1,0:T(8,128)(2,1)} %get-tuple-element.8), calls=%async_computation.12 | async-start | bytes 1048576 | tf_op jit(solution)/shard_map/all_to_all | solution.py:178
  189.4 21.8 %all-to-all-start.8 = ((bf16[16,8,32,128]{3,2,1,0:T(8,128)(2,1)}), bf16[16,8,32,128]{3,2,1,0:T(8,128)(2,1)S(1)}, u32[]{:S(2)}, u32[]{:S(2)}) async-start(bf16[16,8,32,128]{3,2,1,0:T(8,128)(2,1)} %get-tuple-element.6), calls=%async_computation.8 | async-start | bytes 2097152 | tf_op jit(solution)/shard_map/all_to_all | solution.py:178
  211.2 10.4 %all-to-all-start.13 = ((bf16[8,16,512]{2,1,0:T(8,128)(2,1)}), bf16[8,16,512]{2,1,0:T(8,128)(2,1)S(1)}, u32[]{:S(2)}, u32[]{:S(2)}) async-start(bf16[8,16,512]{2,1,0:T(8,128)(2,1)} %reshape.96), calls=%async_computation.13 | async-start | bytes 262144 | tf_op jit(solution)/shard_map/all_to_all | solution.py:178
  221.5 19.2 %all-to-all-start.9 = ((bf16[8,128,512]{2,1,0:T(8,128)(2,1)}), bf16[8,128,512]{2,1,0:T(8,128)(2,1)}, u32[]{:S(2)}, u32[]{:S(2)}) async-start(bf16[8,128,512]{2,1,0:T(8,128)(2,1)} %reshape.92), calls=%async_computation.9 | async-start | bytes 2097152 | tf_op jit(solution)/shard_map/all_to_all | solution.py:178

commit v2 on v1

v2 whole, which is shorter than its diff:
```python
import math

import jax
import jax.numpy as jnp
from jax import lax
from jax.experimental import pallas as pl
from jax.experimental.pallas import tpu as pltpu
from jax.sharding import PartitionSpec as P

H = 32
HD = 128
LAYERS = 8
N_SEC = LAYERS
N_CTX = 16
TOK_DEV = 128
WIDTH = H * HD
HEADS_SEC = H // N_SEC
WIDE = HEADS_SEC * HD
QUARTERS = N_CTX // HEADS_SEC
ROWS = TOK_DEV // QUARTERS
TOK_SEC = TOK_DEV // N_SEC
NQ = N_CTX * ROWS
NK = N_CTX * TOK_DEV
CHUNKS = 4
CK = NK // CHUNKS
CQ = NQ // CHUNKS
LAG = 2

masked_score = -1e30
norm_eps = 1e-06
factor = 1.0 / math.sqrt(HD)
log2e = math.log2(math.e)

NT = (((1,), (1,)), ((), ()))
NN = (((1,), (0,)), ((), ()))
BF16, F32 = jnp.bfloat16, jnp.float32


def dot(a, b, dims):
    return lax.dot_general(a, b, dims, preferred_element_type=jnp.float32)


def add_from(total, part, first):
    if total is None:
        return part
    if first == 0:
        return total + part
    return jnp.concatenate([total[:, :first], total[:, first:] + part], axis=1)


def max_from(total, part, first):
    if total is None:
        return part
    return jnp.concatenate([total[:, :first], jnp.maximum(total[:, first:], part)], axis=1)


def pick(wanted, options):
    chosen = options[0][1]
    for number, option in options[1:]:
        chosen = lax.select(number == wanted, option, chosen)
    return chosen


def cut(index, size):
    return pl.ds(pl.multiple_of(index * size, size), size)


def kernel(
    place_ref,
    x_hbm,
    gain_hbm,
    keys_hbm,
    values_hbm,
    top_hbm,
    grads_out,
    dk_out,
    dv_out,
    k1,
    v1,
    x1,
    gain1,
    top2,
    k2,
    v2,
    x2,
    xw,
    k_ref,
    v_ref,
    kt_ref,
    s_ref,
    dp_ref,
    g_ref,
    dk_ref,
    dv_ref,
    g1,
    y1,
    dk1,
    dv1,
    dk2,
    dv2,
    dk3,
    dv3,
    send,
    recv,
    gain_send,
    gain_recv,
    x1_recv,
    x2_send,
    x2_recv,
    g1_send,
    g1_recv,
    g2_send,
):
    c, s = lax.axis_index("ctx"), lax.axis_index("section")
    head, quarter = c // QUARTERS, c % QUARTERS

    def ctx_at(k):
        y = (c // 4 + k // 4) % 4
        x_lo = (c // 2 + k // 2) % 2
        return y * 4 + x_lo * 2 + (c + k) % 2

    def sec_at(k):
        return ((s // 2 + k // 2) % 4) * 2 + (s + k) % 2

    def away(source, target, send_sem, recv_sem, device):
        return pltpu.make_async_remote_copy(
            src_ref=source,
            dst_ref=target,
            send_sem=send_sem,
            recv_sem=recv_sem,
            device_id=device,
            device_id_type=pl.DeviceIdType.MESH,
        )

    def wait_for(ref, sem):
        pltpu.make_async_copy(ref, ref, sem).wait()

    def each(count, step):
        def run(k, carry):
            step(k)
            return carry

        lax.fori_loop(1, count, run, 0)

    barrier = pltpu.get_barrier_semaphore()

    def greet_ctx(k):
        pl.semaphore_signal(
            barrier, inc=1, device_id=(ctx_at(k), s), device_id_type=pl.DeviceIdType.MESH
        )

    def greet_sec(k):
        pl.semaphore_signal(
            barrier, inc=1, device_id=(c, sec_at(k)), device_id_type=pl.DeviceIdType.MESH
        )

    each(N_SEC, greet_sec)
    each(N_CTX, greet_ctx)
    pl.semaphore_wait(barrier, N_SEC + N_CTX - 2)

    def send_kv1(k):
        to = sec_at(k)
        for n, (source, target) in enumerate(((keys_hbm, k1), (values_hbm, v1))):
            away(
                source.at[:, cut(to, WIDE)],
                target.at[cut(s, TOK_SEC), :],
                send.at[n],
                recv.at[n],
                (c, to),
            ).start()

    each(N_SEC, send_kv1)
    for n, (source, target) in enumerate(((keys_hbm, k1), (values_hbm, v1))):
        pltpu.make_async_copy(
            source.at[:, cut(s, WIDE)], target.at[cut(s, TOK_SEC), :], recv.at[n]
        ).start()

    def send_gain(k):
        to = sec_at(k)
        away(
            gain_hbm.at[:, cut(to * HEADS_SEC + head, HD)],
            gain1.at[s],
            gain_send.at[k],
            gain_recv.at[s],
            (c, to),
        ).start()

    each(N_SEC, send_gain)
    pltpu.make_async_copy(
        gain_hbm.at[:, cut(s * HEADS_SEC + head, HD)], gain1.at[s], gain_recv.at[s]
    ).start()

    def send_x1(k):
        to = sec_at(k)
        away(
            x_hbm.at[0, :, cut(to, WIDE)], x1.at[s], send.at[2], x1_recv.at[s], (c, to)
        ).start()

    each(N_SEC, send_x1)
    pltpu.make_async_copy(x_hbm.at[0, :, cut(s, WIDE)], x1.at[s], x1_recv.at[s]).start()

    def send_top(k):
        to = ctx_at(k)
        away(
            top_hbm.at[cut(to % QUARTERS, ROWS), cut(s * HEADS_SEC + to // QUARTERS, HD)],
            top2.at[c],
            send.at[3],
            recv.at[3],
            (to, s),
        ).start()

    each(N_CTX, send_top)
    pltpu.make_async_copy(
        top_hbm.at[cut(quarter, ROWS), cut(s * HEADS_SEC + head, HD)], top2.at[c], recv.at[3]
    ).start()

    places = [place_ref[b] for b in range(N_CTX)]

    def in_order(ref, target, size, kind):
        blocks = [(places[b], ref[b]) for b in range(N_CTX)]
        for p in range(N_CTX):
            target[p * size : (p + 1) * size, :] = pick(p, blocks).astype(kind)

    def in_blocks(ref, size, target, at):
        sorted_rows = [(p, ref[p * size : (p + 1) * size, :].astype(BF16)) for p in range(N_CTX)]
        for b in range(N_CTX):
            target[(*at, b)] = pick(places[b], sorted_rows)

    wait_for(k1, recv.at[0])
    wait_for(v1, recv.at[1])

    def send_kv2(k):
        to = ctx_at(k)
        for n, (source, target) in enumerate(((k1, k2), (v1, v2))):
            away(
                source.at[:, cut(to // QUARTERS, HD)],
                target.at[c],
                send.at[4 + n],
                recv.at[4 + n],
                (to, s),
            ).start()

    each(N_CTX, send_kv2)
    for n, (source, target) in enumerate(((k1, k2), (v1, v2))):
        pltpu.make_async_copy(
            source.at[:, cut(head, HD)], target.at[c], recv.at[4 + n]
        ).start()

    def pass_x(step, carry):
        layer = LAYERS - 1 - step
        wait_for(x1.at[layer], x1_recv.at[layer])

        def send_x2(k):
            to = ctx_at(k)
            away(
                x1.at[layer, cut(to % QUARTERS, ROWS), cut(to // QUARTERS, HD)],
                x2.at[layer, c],
                x2_send.at[layer],
                x2_recv.at[layer],
                (to, s),
            ).start()

        each(N_CTX, send_x2)
        pltpu.make_async_copy(
            x1.at[layer, cut(quarter, ROWS), cut(head, HD)], x2.at[layer, c], x2_recv.at[layer]
        ).start()
        return carry

    lax.fori_loop(0, LAYERS, pass_x, 0)

    wait_for(top2, recv.at[3])
    in_order(top2, g_ref, ROWS, F32)
    dk_ref[...] = jnp.zeros_like(dk_ref)
    dv_ref[...] = jnp.zeros_like(dv_ref)
    for layer in range(LAYERS):
        wait_for(gain1.at[layer], gain_recv.at[layer])
    wait_for(k2, recv.at[4])
    in_order(k2, k_ref, TOK_DEV, BF16)
    for j in range(CHUNKS):
        rows = slice(j * CK, (j + 1) * CK)
        kt_ref[:, rows] = jnp.transpose(k_ref[rows, :])
    wait_for(v2, recv.at[5])
    in_order(v2, v_ref, TOK_DEV, BF16)

    lane = lax.broadcasted_iota(jnp.int32, (1, CQ), 1)
    query_at = (lane // ROWS) * TOK_DEV + quarter * ROWS + lane % ROWS
    key_at = lax.broadcasted_iota(jnp.int32, (CK, CQ), 0)

    def send_g2(layer):
        wait_for(y1.at[layer], g1_recv.at[layer])

        @pl.when(layer != s)
        def _():
            away(
                y1.at[layer],
                grads_out.at[:, cut(s, WIDE)],
                g2_send.at[layer],
                recv.at[6],
                (c, layer),
            ).start()

        @pl.when(layer == s)
        def _():
            pltpu.make_async_copy(y1.at[layer], grads_out.at[:, cut(s, WIDE)], recv.at[6]).start()

    def one_layer(step, carry):
        layer = LAYERS - 1 - step
        wait_for(x2.at[layer], x2_recv.at[layer])
        in_order(x2.at[layer], xw, ROWS, F32)
        xf = xw[...]
        gain = gain1[layer]
        inv_rms = lax.rsqrt(jnp.mean(xf * xf, axis=1, keepdims=True) + norm_eps)
        query = (xf * inv_rms * gain).astype(BF16)
        grad = g_ref[...].astype(BF16)
        seen = key_at <= query_at

        row_max = None
        for j in range(CHUNKS):
            rows, first = slice(j * CK, (j + 1) * CK), j * CQ
            scores = dot(k_ref[rows, :], query[first:, :], NT)
            diag = jnp.where(seen, scores[:, :CQ], masked_score)
            s_ref[rows, first : first + CQ] = diag
            top = jnp.max(diag, axis=0, keepdims=True)
            if j < CHUNKS - 1:
                s_ref[rows, first + CQ :] = scores[:, CQ:]
                rest = jnp.max(scores[:, CQ:], axis=0, keepdims=True)
                top = jnp.concatenate([top, rest], axis=1)
            row_max = max_from(row_max, top, first)

        total = None
        for j in range(CHUNKS):
            rows, first = slice(j * CK, (j + 1) * CK), j * CQ
            e = jnp.exp2((s_ref[rows, first:] - row_max[:, first:]) * (factor * log2e))
            s_ref[rows, first:] = e
            total = add_from(total, jnp.sum(e, axis=0, keepdims=True), first)
        inv_total = 1.0 / total

        delta = None
        for j in range(CHUNKS):
            rows, first = slice(j * CK, (j + 1) * CK), j * CQ
            dp = dot(v_ref[rows, :], grad[first:, :], NT)
            dp_ref[rows, first:] = dp
            probs = s_ref[rows, first:] * inv_total[:, first:]
            s_ref[rows, first:] = probs
            low = probs.astype(BF16)
            part = jnp.sum(low.astype(F32) * dp, axis=0, keepdims=True)
            delta = add_from(delta, part, first)
            dv_ref[rows, :] += dot(low, grad[first:, :], NN)

        dq_t = None
        for j in range(CHUNKS):
            rows, first = slice(j * CK, (j + 1) * CK), j * CQ
            ds = s_ref[rows, first:] * (dp_ref[rows, first:] - delta[:, first:])
            ds = ds.astype(BF16)
            dk_ref[rows, :] += dot(ds, query[first:, :], NN)
            dq_t = add_from(dq_t, dot(kt_ref[:, rows], ds, NN), first)
        scaled = jnp.transpose(dq_t) * (gain * factor)
        inner = jnp.mean(scaled * xf, axis=1, keepdims=True)
        g_ref[...] += inv_rms * scaled - xf * (inv_rms * inv_rms * inv_rms) * inner
        in_blocks(g_ref, ROWS, g1, (layer,))

        def send_g1(k):
            to = ctx_at(k)
            away(
                g1.at[layer, to],
                y1.at[layer, cut(quarter, ROWS), cut(head, HD)],
                g1_send.at[layer],
                g1_recv.at[layer],
                (to, s),
            ).start()

        each(N_CTX, send_g1)
        pltpu.make_async_copy(
            g1.at[layer, c], y1.at[layer, cut(quarter, ROWS), cut(head, HD)], g1_recv.at[layer]
        ).start()

        @pl.when(step >= LAG)
        def _():
            send_g2(layer + LAG)

        return carry

    lax.fori_loop(0, LAYERS, one_layer, 0)

    dk_ref[...] = dk_ref[...] * factor
    in_blocks(dk_ref, TOK_DEV, dk1, ())
    in_blocks(dv_ref, TOK_DEV, dv1, ())

    def send_dkv(k):
        to = ctx_at(k)
        for n, (source, target) in enumerate(((dk1, dk2), (dv1, dv2))):
            away(source.at[to], target.at[c], send.at[7 + n], recv.at[7 + n], (to, s)).start()

    each(N_CTX, send_dkv)
    for n, (source, target) in enumerate(((dk1, dk2), (dv1, dv2))):
        pltpu.make_async_copy(source.at[c], target.at[c], recv.at[7 + n]).start()

    for layer in range(LAG - 1, -1, -1):
        send_g2(layer)

    for n, (part, whole, out) in enumerate(((dk2, dk3, dk_out), (dv2, dv3, dv_out))):
        wait_for(part, recv.at[7 + n])
        for h in range(HEADS_SEC):
            total = part[h * QUARTERS].astype(F32)
            for q in range(1, QUARTERS):
                total = total + part[h * QUARTERS + q].astype(F32)
            whole[:, h * HD : (h + 1) * HD] = total.astype(BF16)

        def send_whole(k):
            to = sec_at(k)
            away(
                whole.at[cut(to, TOK_SEC), :],
                out.at[:, cut(s, WIDE)],
                send.at[9 + n],
                recv.at[9 + n],
                (c, to),
            ).start()

        each(N_SEC, send_whole)
        pltpu.make_async_copy(
            whole.at[cut(s, TOK_SEC), :], out.at[:, cut(s, WIDE)], recv.at[9 + n]
        ).start()

    wait_for(grads_out, recv.at[6])
    wait_for(dk_out, recv.at[9])
    wait_for(dv_out, recv.at[10])
    for n, ref in enumerate((k1, v1)):
        wait_for(ref.at[pl.ds(0, TOK_DEV - TOK_SEC), :], send.at[n])
    wait_for(x1.at[pl.ds(0, N_SEC - 1)], send.at[2])
    wait_for(top2.at[pl.ds(0, N_CTX - 1)], send.at[3])
    for n, ref in enumerate((k2, v2)):
        wait_for(ref.at[pl.ds(0, N_CTX - 1)], send.at[4 + n])
    for n, ref in enumerate((dk2, dv2)):
        wait_for(ref.at[pl.ds(0, N_CTX - 1)], send.at[7 + n])
    for n, ref in enumerate((dk3, dv3)):
        wait_for(ref.at[pl.ds(0, TOK_DEV - TOK_SEC), :], send.at[9 + n])

    def left(layer, carry):
        wait_for(x2.at[layer, pl.ds(0, N_CTX - 1)], x2_send.at[layer])
        wait_for(g1.at[layer, pl.ds(0, N_CTX - 1)], g1_send.at[layer])

        @pl.when(layer != s)
        def _():
            wait_for(y1.at[layer], g2_send.at[layer])

        return carry

    lax.fori_loop(0, LAYERS, left, 0)
    for k in range(1, N_SEC):
        wait_for(gain1.at[0], gain_send.at[k])


def body(x_saved, gains, keys, values, grad_top, block_order):
    smem = pl.BlockSpec(memory_space=pltpu.SMEM)
    anywhere = pl.BlockSpec(memory_space=pl.ANY)
    dma = pltpu.SemaphoreType.DMA
    grads, dk, dv = pl.pallas_call(
        kernel,
        out_shape=(
            jax.ShapeDtypeStruct((TOK_DEV, WIDTH), BF16),
            jax.ShapeDtypeStruct((TOK_SEC, WIDTH), BF16),
            jax.ShapeDtypeStruct((TOK_SEC, WIDTH), BF16),
        ),
        in_specs=[smem] + [anywhere] * 5,
        out_specs=(anywhere,) * 3,
        scratch_shapes=[
            pltpu.VMEM((TOK_DEV, WIDE), BF16),
            pltpu.VMEM((TOK_DEV, WIDE), BF16),
            pltpu.VMEM((LAYERS, TOK_DEV, WIDE), BF16),
            pltpu.VMEM((LAYERS, 1, HD), F32),
            pltpu.VMEM((N_CTX, ROWS, HD), BF16),
            pltpu.VMEM((N_CTX, TOK_DEV, HD), BF16),
            pltpu.VMEM((N_CTX, TOK_DEV, HD), BF16),
            pltpu.VMEM((LAYERS, N_CTX, ROWS, HD), BF16),
            pltpu.VMEM((NQ, HD), F32),
            pltpu.VMEM((NK, HD), BF16),
            pltpu.VMEM((NK, HD), BF16),
            pltpu.VMEM((HD, NK), BF16),
            pltpu.VMEM((NK, NQ), F32),
            pltpu.VMEM((NK, NQ), F32),
            pltpu.VMEM((NQ, HD), F32),
            pltpu.VMEM((NK, HD), F32),
            pltpu.VMEM((NK, HD), F32),
            pltpu.VMEM((LAYERS, N_CTX, ROWS, HD), BF16),
            pltpu.VMEM((LAYERS, TOK_DEV, WIDE), BF16),
            pltpu.VMEM((N_CTX, TOK_DEV, HD), BF16),
            pltpu.VMEM((N_CTX, TOK_DEV, HD), BF16),
            pltpu.VMEM((N_CTX, TOK_DEV, HD), BF16),
            pltpu.VMEM((N_CTX, TOK_DEV, HD), BF16),
            pltpu.VMEM((TOK_DEV, WIDE), BF16),
            pltpu.VMEM((TOK_DEV, WIDE), BF16),
            dma((11,)),
            dma((11,)),
            dma((N_SEC,)),
            dma((N_SEC,)),
            dma((LAYERS,)),
            dma((LAYERS,)),
            dma((LAYERS,)),
            dma((LAYERS,)),
            dma((LAYERS,)),
            dma((LAYERS,)),
        ],
        compiler_params=pltpu.CompilerParams(
            vmem_limit_bytes=56 * 2**20, collective_id=0, has_side_effects=True
        ),
    )(block_order, x_saved, gains, keys, values, grad_top)
    return (grads.astype(F32)[None], dk.astype(F32), dv.astype(F32))


def solution(mesh):
    placed = (
        P("section", "ctx", None),
        P("section", None),
        P(("ctx", "section"), None),
        P(("ctx", "section"), None),
        P("ctx", None),
        P(),
    )
    return jax.shard_map(
        body,
        mesh=mesh,
        in_specs=placed,
        out_specs=(
            P("section", "ctx", None),
            P(("ctx", "section"), None),
            P(("ctx", "section"), None),
        ),
        check_vma=False,
    )
```

time: 250 us -> 102 us (0.41); the launches traced: 247 us -> 102 us
  waiting for transfers between devices: 113 us -> 0 us
  Pallas kernels: 26.3 us -> 96.7 us
  starting transfers between devices: 60.6 us -> 0 us
  blocking collectives: 23.5 us -> 0 us
  local copies, waits for them, and re-layouts: 20.5 us -> 0.01 us
    all_to_all x12 -> x0, waiting for transfers between devices: 113 us -> none  [swap(): return lax.all_to_all(value, axis, split_axis=0, concat_axis=0, tiled=True)]
    pallas_call x1, Pallas kernels: 26.3 us -> 96.7 us  [body(): pl.pallas_call(kernel, out_shape=(jax.ShapeDtypeStruct((TOK_DEV, WIDTH),...]
    all_to_all x12 -> x0, starting transfers between devices: 60.6 us -> none  [swap(): return lax.all_to_all(value, axis, split_axis=0, concat_axis=0, tiled=True)]
    all_to_all x2 -> x0, blocking collectives: 23.5 us -> none  [swap(): return lax.all_to_all(value, axis, split_axis=0, concat_axis=0, tiled=True)]
    reshape x10 -> x0, local copies, waits for them, and re-layouts: 6.32 us -> none  [the longest x2 3.14 us: spread(): value = swap(value.reshape(-1, n_sec, wide).transpose(1, 0, 2), 'section')]
    unnamed x14 -> x4, local copies, waits for them, and re-layouts: 5.06 us -> 0.01 us
    convert_element_type x3 -> x0, local copies, waits for them, and re-layouts: 3.27 us -> none  [the longest x1 1.83 us: body(): g = g.transpose(1, 0, 2).reshape(1, TOK_DEV, H * HD).astype(jnp.float32)]
    broadcast_in_dim x0 -> x1, other arithmetic: none -> 2.8 us  [body(): return (grads.astype(F32)[None], dk.astype(F32), dv.astype(F32))]
  transfers between devices with their start and end apart: 12 -> 0, of which waited for: 12 -> 0; matrix products, arithmetic and copies ran while one was open for 5% -> 0% of each run, Pallas kernels for 0% -> 0%
where the time goes in v2:
time: 102 us
  Pallas kernels  96.7 us (95%)
  other arithmetic  4.24 us (4%)
    pallas_call x1, Pallas kernels, body(): pl.pallas_call(kernel, out_shape=(jax.ShapeDtypeStruct((TOK_DEV, WIDTH),...  96.7 us
    broadcast_in_dim x1, other arithmetic, body(): return (grads.astype(F32)[None], dk.astype(F32), dv.astype(F32))  2.8 us

profile of v2, /device:TPU:1, one launch (start us, length us, event | category | flops | bytes accessed | tf_op | source)
XLA Modules:
  0.0 101.6 jit_solution(15580707145850330127)
XLA Ops:
  0.6 96.7 %shard_map.85 = (bf16[128,4096]{1,0:T(8,128)(2,1)}, bf16[16,4096]{1,0:T(8,128)(2,1)}, bf16[16,4096]{1,0:T(8,128)(2,1)}) custom-call(s32[16]{0:T(128)} %place_ref.1, bf16[1,128,4096]{2,1,0:T(8,128)(2,1)} %x_hbm.1, f32[1,4096]{1,0:T(1,128)} %gain_hbm.1, bf16[16,4096]{1,0:T(8,128)(2,1)} %keys_hbm.1, bf16[16,4096]{1,0:T(8,128)(2,1)} %values_hbm.1, ...), custom_call_target="tpu_custom_call" | custom-call | tf_op jit(solution)/shard_map/pallas_call | solution.py:457
  97.3 0.0 copy-start.1
  97.3 0.0 copy-start
  97.3 2.8 %bitcast_convert_fusion = f32[1,128,4096]{2,1,0:T(8,128)} fusion(bf16[128,4096]{1,0:T(8,128)(2,1)} %get-tuple-element.6), kind=kLoop, calls=%fused_computation | loop fusion | flops 524288 | bytes 3145728 | tf_op jit(solution)/shard_map/broadcast_in_dim | solution.py:507
  100.1 0.0 copy-done.1
  100.1 0.7 convert_element_type.7
  100.9 0.0 copy-done
  100.9 0.7 convert_element_type.8
Async XLA Ops:
  97.3 2.8 %copy-start.1 = (bf16[16,4096]{1,0:T(8,128)(2,1)S(1)}, bf16[16,4096]{1,0:T(8,128)(2,1)}, u32[]{:S(2)}) copy-start(bf16[16,4096]{1,0:T(8,128)(2,1)} %get-tuple-element.7) | copy-start | bytes 393220
  97.3 3.5 %copy-start = (bf16[16,4096]{1,0:T(8,128)(2,1)S(1)}, bf16[16,4096]{1,0:T(8,128)(2,1)}, u32[]{:S(2)}) copy-start(bf16[16,4096]{1,0:T(8,128)(2,1)} %get-tuple-element.8) | copy-start | bytes 393220

commit v3 on v2

v3 whole, which is shorter than its diff:
```python
import math

import jax
import jax.numpy as jnp
from jax import lax
from jax.experimental import pallas as pl
from jax.experimental.pallas import tpu as pltpu
from jax.sharding import PartitionSpec as P

H = 32
HD = 128
LAYERS = 8
N_SEC = LAYERS
N_CTX = 16
TOK_DEV = 128
WIDTH = H * HD
HEADS_SEC = H // N_SEC
WIDE = HEADS_SEC * HD
N_NEAR = N_CTX // 2
ROWS = TOK_DEV // 2
TOK_SEC = TOK_DEV // N_SEC
NQ = N_NEAR * ROWS
NK = N_CTX * TOK_DEV
PART = 32
PARTS = (0, 2, 1, 3)
CHUNKS = (
    (slice(0, 512), 0),
    (slice(512, 1024), 0),
    (slice(1024, 1280), 0),
    (slice(1280, 1536), 128),
    (slice(1536, 1792), 256),
    (slice(1792, 2048), 384),
)
LAG = 2

masked_score = -1e30
norm_eps = 1e-06
factor = 1.0 / math.sqrt(HD)
log2e = math.log2(math.e)

NT = (((1,), (1,)), ((), ()))
NN = (((1,), (0,)), ((), ()))
BF16, F32 = jnp.bfloat16, jnp.float32


def dot(a, b, dims):
    return lax.dot_general(a, b, dims, preferred_element_type=jnp.float32)


def add_from(total, part, first):
    if total is None:
        return part
    if first == 0:
        return total + part
    return jnp.concatenate([total[:, :first], total[:, first:] + part], axis=1)


def max_from(total, part, first):
    if total is None:
        return part
    if first == 0:
        return jnp.maximum(total, part)
    return jnp.concatenate([total[:, :first], jnp.maximum(total[:, first:], part)], axis=1)


def pick(wanted, options):
    chosen = options[0][1]
    for number, option in options[1:]:
        chosen = lax.select(number == wanted, option, chosen)
    return chosen


def cut(index, size):
    return pl.ds(pl.multiple_of(index * size, size), size)


def kernel(
    place_ref,
    x_hbm,
    gain_hbm,
    keys_hbm,
    values_hbm,
    top_hbm,
    grads_out,
    dk_out,
    dv_out,
    k1,
    v1,
    x1,
    gain1,
    top2,
    k2,
    v2,
    x2,
    xw,
    k_ref,
    v_ref,
    kt_ref,
    bias_ref,
    s_ref,
    dp_ref,
    g_ref,
    dk_ref,
    dv_ref,
    g1,
    y1,
    dk1,
    dv1,
    dk2,
    dv2,
    dk3,
    dv3,
    dk4,
    dv4,
    dk5,
    dv5,
    send,
    recv,
    gain_send,
    gain_recv,
    x1_recv,
    x2_send,
    x2_recv,
    g1_send,
    g1_recv,
    g2_send,
):
    c, s = lax.axis_index("ctx"), lax.axis_index("section")
    y, x_lo, core = c // 4, (c // 2) % 2, c % 2
    other = 1 - core
    mine, near = y * 2 + core, y * 2 + x_lo

    def device(to_y, to_x_lo, to_core):
        return (to_y * 4 + to_x_lo * 2 + to_core, s)

    def sec_at(k):
        return ((s // 2 + k // 2) % 4) * 2 + (s + k) % 2

    def away(source, target, send_sem, recv_sem, to):
        return pltpu.make_async_remote_copy(
            src_ref=source,
            dst_ref=target,
            send_sem=send_sem,
            recv_sem=recv_sem,
            device_id=to,
            device_id_type=pl.DeviceIdType.MESH,
        )

    def wait_for(ref, sem):
        pltpu.make_async_copy(ref, ref, sem).wait()

    def each(first, last, step):
        def run(k, carry):
            step(k)
            return carry

        lax.fori_loop(first, last, run, 0)

    barrier = pltpu.get_barrier_semaphore()

    def greet(to):
        pl.semaphore_signal(barrier, inc=1, device_id=to, device_id_type=pl.DeviceIdType.MESH)

    each(1, N_SEC, lambda k: greet((c, sec_at(k))))
    each(1, 4, lambda k: greet(device((y + k) % 4, x_lo, core)))
    each(0, 4, lambda k: greet(device((y + k) % 4, x_lo, other)))
    each(0, 4, lambda k: greet(device((y + k) % 4, 1 - x_lo, core)))
    pl.semaphore_wait(barrier, N_SEC - 1 + 11)

    first_hop = ((keys_hbm, k1), (values_hbm, v1))

    def send_kv1(k):
        to = sec_at(k)
        for n, (source, target) in enumerate(first_hop):
            away(
                source.at[:, cut(to, WIDE)],
                target.at[cut(s, TOK_SEC), :],
                send.at[n],
                recv.at[n],
                (c, to),
            ).start()

    each(1, N_SEC, send_kv1)
    for n, (source, target) in enumerate(first_hop):
        pltpu.make_async_copy(
            source.at[:, cut(s, WIDE)], target.at[cut(s, TOK_SEC), :], recv.at[n]
        ).start()

    def send_gain(k):
        to = sec_at(k)
        away(
            gain_hbm.at[:, cut(to * HEADS_SEC + y, HD)],
            gain1.at[s],
            gain_send.at[k],
            gain_recv.at[s],
            (c, to),
        ).start()

    each(1, N_SEC, send_gain)
    pltpu.make_async_copy(
        gain_hbm.at[:, cut(s * HEADS_SEC + y, HD)], gain1.at[s], gain_recv.at[s]
    ).start()

    for part in PARTS:
        rows = pl.ds(part * PART, PART)

        def send_x1(k):
            to = sec_at(k)
            away(
                x_hbm.at[0, rows, cut(to, WIDE)],
                x1.at[s, rows, :],
                send.at[2],
                x1_recv.at[s, part],
                (c, to),
            ).start()

        each(1, N_SEC, send_x1)
        pltpu.make_async_copy(
            x_hbm.at[0, rows, cut(s, WIDE)], x1.at[s, rows, :], x1_recv.at[s, part]
        ).start()

    def send_top(to_y, to_core):
        away(
            top_hbm.at[cut(to_core, ROWS), cut(s * HEADS_SEC + to_y, HD)],
            top2.at[mine],
            send.at[3],
            recv.at[3],
            device(to_y, x_lo, to_core),
        ).start()

    each(1, 4, lambda k: send_top((y + k) % 4, core))
    each(0, 4, lambda k: send_top((y + k) % 4, other))
    pltpu.make_async_copy(
        top_hbm.at[cut(core, ROWS), cut(s * HEADS_SEC + y, HD)], top2.at[mine], recv.at[3]
    ).start()

    places = [place_ref[b] for b in range(N_CTX)]
    near_places = [place_ref[(e // 2) * 4 + x_lo * 2 + e % 2] for e in range(N_NEAR)]
    ranks = []
    for e in range(N_NEAR):
        rank = 0
        for f in range(N_NEAR):
            if f != e:
                rank = rank + jnp.where(near_places[f] < near_places[e], 1, 0)
        ranks.append(rank)

    def in_order(ref, numbers, target, size, kind):
        blocks = [(number, ref[n]) for n, number in enumerate(numbers)]
        for p in range(len(numbers)):
            target[p * size : (p + 1) * size, :] = pick(p, blocks).astype(kind)

    lane = lax.broadcasted_iota(jnp.int32, (1, NQ), 1)
    query_at = core * ROWS + lane % ROWS
    for e in range(N_NEAR):
        query_at = query_at + jnp.where(lane // ROWS == ranks[e], near_places[e] * TOK_DEV, 0)

    def make_bias(n, carry):
        key_at = lax.broadcasted_iota(jnp.int32, (TOK_DEV, NQ), 0) + n * TOK_DEV
        bias_ref[cut(n, TOK_DEV), :] = jnp.where(key_at <= query_at, 0.0, masked_score)
        return carry

    second_hop = ((k1, k2), (v1, v2))
    wait_for(k1, recv.at[0])
    wait_for(v1, recv.at[1])

    def send_kv2(to_y, to_x_lo):
        for n, (source, target) in enumerate(second_hop):
            away(
                source.at[:, cut(to_y, HD)],
                target.at[core, near],
                send.at[4 + n],
                recv.at[4 + n],
                device(to_y, to_x_lo, core),
            ).start()

    each(0, 4, lambda k: send_kv2((y + k) % 4, 1 - x_lo))
    each(1, 4, lambda k: send_kv2((y + k) % 4, x_lo))
    for n, (source, target) in enumerate(second_hop):
        pltpu.make_async_copy(
            source.at[:, cut(y, HD)], target.at[core, near], recv.at[4 + n]
        ).start()

    def pass_x(part):
        to_core = part // (ROWS // PART)
        rows = pl.ds(part * PART, PART)
        at = pl.ds(part % (ROWS // PART) * PART, PART)

        def one(step, carry):
            layer = LAYERS - 1 - step
            wait_for(x1.at[layer, rows, :], x1_recv.at[layer, part])

            def send_x2(to_y):
                away(
                    x1.at[layer, rows, cut(to_y, HD)],
                    x2.at[layer, mine, at, :],
                    x2_send.at[layer],
                    x2_recv.at[layer],
                    device(to_y, x_lo, to_core),
                ).start()

            each(1, 4, lambda k: send_x2((y + k) % 4))

            @pl.when(core != to_core)
            def _():
                send_x2(y)

            @pl.when(core == to_core)
            def _():
                pltpu.make_async_copy(
                    x1.at[layer, rows, cut(y, HD)], x2.at[layer, mine, at, :], x2_recv.at[layer]
                ).start()

            return carry

        lax.fori_loop(0, LAYERS, one, 0)

    for part in PARTS[:2]:
        pass_x(part)

    for n, ref in enumerate((k2, v2)):
        wait_for(ref.at[core], recv.at[4 + n])
        away(
            ref.at[core], ref.at[core], send.at[6 + n], recv.at[6 + n], device(y, x_lo, other)
        ).start()
    lax.fori_loop(0, N_CTX, make_bias, 0)
    for part in PARTS[2:]:
        pass_x(part)

    wait_for(top2, recv.at[3])
    in_order(top2, ranks, g_ref, ROWS, F32)
    dk_ref[...] = jnp.zeros_like(dk_ref)
    dv_ref[...] = jnp.zeros_like(dv_ref)
    for layer in range(LAYERS):
        wait_for(gain1.at[layer], gain_recv.at[layer])

    wait_for(k2.at[other], recv.at[6])
    wait_for(v2.at[other], recv.at[7])
    for ref, target in ((k2, k_ref), (v2, v_ref)):
        blocks = [(places[b], ref[b % 2, b // 2]) for b in range(N_CTX)]
        for p in range(N_CTX):
            target[p * TOK_DEV : (p + 1) * TOK_DEV, :] = pick(p, blocks)
    for n in range(4):
        rows = slice(n * 512, (n + 1) * 512)
        kt_ref[:, rows] = jnp.transpose(k_ref[rows, :])

    def send_g2(layer):
        wait_for(y1.at[layer], g1_recv.at[layer])

        @pl.when(layer != s)
        def _():
            away(
                y1.at[layer],
                grads_out.at[:, cut(s, WIDE)],
                g2_send.at[layer],
                recv.at[8],
                (c, layer),
            ).start()

        @pl.when(layer == s)
        def _():
            pltpu.make_async_copy(y1.at[layer], grads_out.at[:, cut(s, WIDE)], recv.at[8]).start()

    def one_layer(step, carry):
        layer = LAYERS - 1 - step
        wait_for(x2.at[layer], x2_recv.at[layer])
        in_order(x2.at[layer], ranks, xw, ROWS, F32)
        xf = xw[...]
        gain = gain1[layer]
        inv_rms = lax.rsqrt(jnp.mean(xf * xf, axis=1, keepdims=True) + norm_eps)
        query = (xf * inv_rms * gain).astype(BF16)
        grad = g_ref[...].astype(BF16)

        row_max = None
        for rows, first in CHUNKS:
            scores = dot(k_ref[rows, :], query[first:, :], NT) + bias_ref[rows, first:]
            s_ref[rows, first:] = scores
            row_max = max_from(row_max, jnp.max(scores, axis=0, keepdims=True), first)

        total = None
        for rows, first in CHUNKS:
            e = jnp.exp2((s_ref[rows, first:] - row_max[:, first:]) * (factor * log2e))
            s_ref[rows, first:] = e
            total = add_from(total, jnp.sum(e, axis=0, keepdims=True), first)
        inv_total = 1.0 / total

        delta = None
        for rows, first in CHUNKS:
            dp = dot(v_ref[rows, :], grad[first:, :], NT)
            dp_ref[rows, first:] = dp
            probs = s_ref[rows, first:] * inv_total[:, first:]
            s_ref[rows, first:] = probs
            low = probs.astype(BF16)
            part = jnp.sum(low.astype(F32) * dp, axis=0, keepdims=True)
            delta = add_from(delta, part, first)
            dv_ref[rows, :] += dot(low, grad[first:, :], NN)

        dq_t = None
        for rows, first in CHUNKS:
            ds = s_ref[rows, first:] * (dp_ref[rows, first:] - delta[:, first:])
            ds = ds.astype(BF16)
            dk_ref[rows, :] += dot(ds, query[first:, :], NN)
            dq_t = add_from(dq_t, dot(kt_ref[:, rows], ds, NN), first)
        scaled = jnp.transpose(dq_t) * (gain * factor)
        inner = jnp.mean(scaled * xf, axis=1, keepdims=True)
        g_ref[...] += inv_rms * scaled - xf * (inv_rms * inv_rms * inv_rms) * inner
        by_rank = [(r, g_ref[r * ROWS : (r + 1) * ROWS, :].astype(BF16)) for r in range(N_NEAR)]
        for e in range(N_NEAR):
            g1[layer, e] = pick(ranks[e], by_rank)

        def send_g1(to_y, to_core):
            away(
                g1.at[layer, to_y * 2 + to_core],
                y1.at[layer, cut(core, ROWS), cut(y, HD)],
                g1_send.at[layer],
                g1_recv.at[layer],
                device(to_y, x_lo, to_core),
            ).start()

        each(1, 4, lambda k: send_g1((y + k) % 4, core))
        each(0, 4, lambda k: send_g1((y + k) % 4, other))
        pltpu.make_async_copy(
            g1.at[layer, mine], y1.at[layer, cut(core, ROWS), cut(y, HD)], g1_recv.at[layer]
        ).start()

        @pl.when(step >= LAG)
        def _():
            send_g2(layer + LAG)

        return carry

    lax.fori_loop(0, LAYERS, one_layer, 0)

    dk_ref[...] = dk_ref[...] * factor
    sums = (
        (dk_ref, dk1, dk2, dk3, dk4, dk5, dk_out),
        (dv_ref, dv1, dv2, dv3, dv4, dv5, dv_out),
    )

    def in_blocks(ref, of_core, kind):
        by_place = [
            (p, ref[p * TOK_DEV : (p + 1) * TOK_DEV, :].astype(kind)) for p in range(N_CTX)
        ]
        for f in range(N_NEAR):
            yield f, pick(place_ref[f * 2 + of_core], by_place)

    for n, (ref, part1, part2, _, _, _, _) in enumerate(sums):
        for f, rows in in_blocks(ref, other, BF16):
            part1[f] = rows
        away(part1, part2, send.at[8 + n], recv.at[9 + n], device(y, x_lo, other)).start()

    for n, (ref, _, part2, part3, part4, _, _) in enumerate(sums):
        wait_for(part2, recv.at[9 + n])
        for f, rows in in_blocks(ref, core, F32):
            part3[f] = (rows + part2[f].astype(F32)).astype(BF16)

        def send_sum(to_y, to_x_lo):
            away(
                part3.at[to_y * 2 + to_x_lo],
                part4.at[near],
                send.at[10 + n],
                recv.at[11 + n],
                device(to_y, to_x_lo, core),
            ).start()

        each(0, 4, lambda k: send_sum((y + k) % 4, 1 - x_lo))
        each(1, 4, lambda k: send_sum((y + k) % 4, x_lo))
        pltpu.make_async_copy(part3.at[near], part4.at[near], recv.at[11 + n]).start()

    for layer in range(LAG - 1, -1, -1):
        send_g2(layer)

    for n, (_, _, _, _, part4, part5, out) in enumerate(sums):
        wait_for(part4, recv.at[11 + n])
        for h in range(HEADS_SEC):
            both = part4[h * 2].astype(F32) + part4[h * 2 + 1].astype(F32)
            part5[:, h * HD : (h + 1) * HD] = both.astype(BF16)

        def send_whole(k):
            to = sec_at(k)
            away(
                part5.at[cut(to, TOK_SEC), :],
                out.at[:, cut(s, WIDE)],
                send.at[12 + n],
                recv.at[13 + n],
                (c, to),
            ).start()

        each(1, N_SEC, send_whole)
        pltpu.make_async_copy(
            part5.at[cut(s, TOK_SEC), :], out.at[:, cut(s, WIDE)], recv.at[13 + n]
        ).start()

    wait_for(grads_out, recv.at[8])
    wait_for(dk_out, recv.at[13])
    wait_for(dv_out, recv.at[14])
    most = pl.ds(0, N_SEC - 1)
    for n, ref in enumerate((k1, v1)):
        wait_for(ref.at[pl.ds(0, TOK_DEV - TOK_SEC), :], send.at[n])
    wait_for(x1.at[most], send.at[2])
    wait_for(top2.at[most], send.at[3])
    for n, ref in enumerate((k2, v2)):
        wait_for(ref.at[0, most], send.at[4 + n])
        wait_for(ref.at[0], send.at[6 + n])
    for n, (_, part1, _, part3, _, part5, _) in enumerate(sums):
        wait_for(part1, send.at[8 + n])
        wait_for(part3.at[most], send.at[10 + n])
        wait_for(part5.at[pl.ds(0, TOK_DEV - TOK_SEC), :], send.at[12 + n])

    def left(layer, carry):
        wait_for(x2.at[layer, most], x2_send.at[layer])
        wait_for(g1.at[layer, most], g1_send.at[layer])

        @pl.when(layer != s)
        def _():
            wait_for(y1.at[layer], g2_send.at[layer])

        return carry

    lax.fori_loop(0, LAYERS, left, 0)
    for k in range(1, N_SEC):
        wait_for(gain1.at[0], gain_send.at[k])


def body(x_saved, gains, keys, values, grad_top, block_order):
    smem = pl.BlockSpec(memory_space=pltpu.SMEM)
    anywhere = pl.BlockSpec(memory_space=pl.ANY)
    dma = pltpu.SemaphoreType.DMA
    grads, dk, dv = pl.pallas_call(
        kernel,
        out_shape=(
            jax.ShapeDtypeStruct((TOK_DEV, WIDTH), BF16),
            jax.ShapeDtypeStruct((TOK_SEC, WIDTH), BF16),
            jax.ShapeDtypeStruct((TOK_SEC, WIDTH), BF16),
        ),
        in_specs=[smem] + [anywhere] * 5,
        out_specs=(anywhere,) * 3,
        scratch_shapes=[
            pltpu.VMEM((TOK_DEV, WIDE), BF16),
            pltpu.VMEM((TOK_DEV, WIDE), BF16),
            pltpu.VMEM((LAYERS, TOK_DEV, WIDE), BF16),
            pltpu.VMEM((LAYERS, 1, HD), F32),
            pltpu.VMEM((N_NEAR, ROWS, HD), BF16),
            pltpu.VMEM((2, N_NEAR, TOK_DEV, HD), BF16),
            pltpu.VMEM((2, N_NEAR, TOK_DEV, HD), BF16),
            pltpu.VMEM((LAYERS, N_NEAR, ROWS, HD), BF16),
            pltpu.VMEM((NQ, HD), F32),
            pltpu.VMEM((NK, HD), BF16),
            pltpu.VMEM((NK, HD), BF16),
            pltpu.VMEM((HD, NK), BF16),
            pltpu.VMEM((NK, NQ), F32),
            pltpu.VMEM((NK, NQ), F32),
            pltpu.VMEM((NK, NQ), F32),
            pltpu.VMEM((NQ, HD), F32),
            pltpu.VMEM((NK, HD), F32),
            pltpu.VMEM((NK, HD), F32),
            pltpu.VMEM((LAYERS, N_NEAR, ROWS, HD), BF16),
            pltpu.VMEM((LAYERS, TOK_DEV, WIDE), BF16),
        ]
        + [pltpu.VMEM((N_NEAR, TOK_DEV, HD), BF16)] * 8
        + [pltpu.VMEM((TOK_DEV, WIDE), BF16)] * 2
        + [
            dma((14,)),
            dma((15,)),
            dma((N_SEC,)),
            dma((N_SEC,)),
            dma((LAYERS, TOK_DEV // PART)),
            dma((LAYERS,)),
            dma((LAYERS,)),
            dma((LAYERS,)),
            dma((LAYERS,)),
            dma((LAYERS,)),
        ],
        compiler_params=pltpu.CompilerParams(
            vmem_limit_bytes=56 * 2**20, collective_id=0, has_side_effects=True
        ),
    )(block_order, x_saved, gains, keys, values, grad_top)
    return (grads.astype(F32)[None], dk.astype(F32), dv.astype(F32))


def solution(mesh):
    placed = (
        P("section", "ctx", None),
        P("section", None),
        P(("ctx", "section"), None),
        P(("ctx", "section"), None),
        P("ctx", None),
        P(),
    )
    return jax.shard_map(
        body,
        mesh=mesh,
        in_specs=placed,
        out_specs=(
            P("section", "ctx", None),
            P(("ctx", "section"), None),
            P(("ctx", "section"), None),
        ),
        check_vma=False,
    )
```

time: 102 us -> 93.9 us (0.921)
  Pallas kernels: 96.7 us -> 88.8 us
    pallas_call x1, Pallas kernels: 96.7 us -> 88.8 us  [body(): pl.pallas_call(kernel, out_shape=(jax.ShapeDtypeStruct((TOK_DEV, WIDTH),...]
where the time goes in v3:
time: 93.9 us; the launch traced here: 93.7 us
  Pallas kernels  88.8 us (95%)
  other arithmetic  4.24 us (5%)
    pallas_call x1, Pallas kernels, body(): pl.pallas_call(kernel, out_shape=(jax.ShapeDtypeStruct((TOK_DEV, WIDTH),...  88.8 us
    broadcast_in_dim x1, other arithmetic, body(): return (grads.astype(F32)[None], dk.astype(F32), dv.astype(F32))  2.8 us

profile of v3, /device:TPU:1, one launch (start us, length us, event | category | flops | bytes accessed | tf_op | source)
XLA Modules:
  0.0 93.7 jit_solution(15081594232666978427)
XLA Ops:
  0.6 88.8 %shard_map.85 = (bf16[128,4096]{1,0:T(8,128)(2,1)}, bf16[16,4096]{1,0:T(8,128)(2,1)}, bf16[16,4096]{1,0:T(8,128)(2,1)}) custom-call(s32[16]{0:T(128)} %place_ref.1, bf16[1,128,4096]{2,1,0:T(8,128)(2,1)} %x_hbm.1, f32[1,4096]{1,0:T(1,128)} %gain_hbm.1, bf16[16,4096]{1,0:T(8,128)(2,1)} %keys_hbm.1, bf16[16,4096]{1,0:T(8,128)(2,1)} %values_hbm.1, ...), custom_call_target="tpu_custom_call" | custom-call | tf_op jit(solution)/shard_map/pallas_call | solution.py:528
  89.5 0.0 copy-start.1
  89.5 0.0 copy-start
  89.5 2.8 %bitcast_convert_fusion = f32[1,128,4096]{2,1,0:T(8,128)} fusion(bf16[128,4096]{1,0:T(8,128)(2,1)} %get-tuple-element.6), kind=kLoop, calls=%fused_computation | loop fusion | flops 524288 | bytes 3145728 | tf_op jit(solution)/shard_map/broadcast_in_dim | solution.py:577
  92.3 0.0 copy-done.1
  92.3 0.7 convert_element_type.7
  93.0 0.0 copy-done
  93.0 0.7 convert_element_type.8
Async XLA Ops:
  89.5 2.8 %copy-start.1 = (bf16[16,4096]{1,0:T(8,128)(2,1)S(1)}, bf16[16,4096]{1,0:T(8,128)(2,1)}, u32[]{:S(2)}) copy-start(bf16[16,4096]{1,0:T(8,128)(2,1)} %get-tuple-element.7) | copy-start | bytes 393220
  89.5 3.5 %copy-start = (bf16[16,4096]{1,0:T(8,128)(2,1)S(1)}, bf16[16,4096]{1,0:T(8,128)(2,1)}, u32[]{:S(2)}) copy-start(bf16[16,4096]{1,0:T(8,128)(2,1)} %get-tuple-element.8) | copy-start | bytes 393220

commit v4 on v3

--- a/solution.py
+++ b/solution.py
@@ -21,8 +21,7 @@
 TOK_SEC = TOK_DEV // N_SEC
 NQ = N_NEAR * ROWS
 NK = N_CTX * TOK_DEV
-PART = 32
-PARTS = (0, 2, 1, 3)
+PART = ROWS // 2
 CHUNKS = (
     (slice(0, 512), 0),
     (slice(512, 1024), 0),
@@ -32,6 +31,7 @@
     (slice(1792, 2048), 384),
 )
 LAG = 2
+WIDEN_STEPS = 4
 
 masked_score = -1e30
 norm_eps = 1e-06
@@ -87,6 +87,7 @@
     k1,
     v1,
     x1,
+    z1,
     gain1,
     top2,
     k2,
@@ -121,6 +122,8 @@
     x1_recv,
     x2_send,
     x2_recv,
+    z1_recv,
+    z2_recv,
     g1_send,
     g1_recv,
     g2_send,
@@ -201,23 +204,48 @@
         gain_hbm.at[:, cut(s * HEADS_SEC + y, HD)], gain1.at[s], gain_recv.at[s]
     ).start()
 
-    for part in PARTS:
-        rows = pl.ds(part * PART, PART)
+    for to_core in range(2):
+        rows = pl.ds(to_core * ROWS, PART)
 
         def send_x1(k):
             to = sec_at(k)
             away(
                 x_hbm.at[0, rows, cut(to, WIDE)],
-                x1.at[s, rows, :],
+                x1.at[s, to_core],
                 send.at[2],
-                x1_recv.at[s, part],
+                x1_recv.at[s, to_core],
                 (c, to),
             ).start()
 
         each(1, N_SEC, send_x1)
         pltpu.make_async_copy(
-            x_hbm.at[0, rows, cut(s, WIDE)], x1.at[s, rows, :], x1_recv.at[s, part]
-        ).start()
+            x_hbm.at[0, rows, cut(s, WIDE)], x1.at[s, to_core], x1_recv.at[s, to_core]
+        ).start()
+
+    def send_z1(k):
+        to_sec = sec_at(k)
+
+        def rows_for(to_y, to_core):
+            return x_hbm.at[
+                0, pl.ds(to_core * ROWS + PART, PART), cut(to_sec * HEADS_SEC + to_y, HD)
+            ]
+
+        def send_to(to_y, to_core):
+            away(
+                rows_for(to_y, to_core),
+                z1.at[to_sec, mine],
+                send.at[14],
+                z1_recv.at[to_sec],
+                device(to_y, x_lo, to_core),
+            ).start()
+
+        each(1, 4, lambda q: send_to((y + q) % 4, core))
+        each(0, 4, lambda q: send_to((y + q) % 4, other))
+        pltpu.make_async_copy(
+            rows_for(y, core), z1.at[to_sec, mine], z1_recv.at[to_sec]
+        ).start()
+
+    each(1, N_SEC + 1, send_z1)
 
     def send_top(to_y, to_core):
         away(
@@ -280,19 +308,29 @@
             source.at[:, cut(y, HD)], target.at[core, near], recv.at[4 + n]
         ).start()
 
-    def pass_x(part):
-        to_core = part // (ROWS // PART)
-        rows = pl.ds(part * PART, PART)
-        at = pl.ds(part % (ROWS // PART) * PART, PART)
-
+    def pass_z(k):
+        to = sec_at(k)
+        wait_for(z1.at[to], z1_recv.at[to])
+        target = x2.at[s, :, pl.ds(PART, PART), :]
+
+        @pl.when(to != s)
+        def _():
+            away(z1.at[to], target, send.at[15], z2_recv.at[s], (c, to)).start()
+
+        @pl.when(to == s)
+        def _():
+            pltpu.make_async_copy(z1.at[to], target, z2_recv.at[s]).start()
+
+    def pass_x(to_core):
         def one(step, carry):
             layer = LAYERS - 1 - step
-            wait_for(x1.at[layer, rows, :], x1_recv.at[layer, part])
+            wait_for(x1.at[layer, to_core], x1_recv.at[layer, to_core])
+            target = x2.at[layer, mine, pl.ds(0, PART), :]
 
             def send_x2(to_y):
                 away(
-                    x1.at[layer, rows, cut(to_y, HD)],
-                    x2.at[layer, mine, at, :],
+                    x1.at[layer, to_core, :, cut(to_y, HD)],
+                    target,
                     x2_send.at[layer],
                     x2_recv.at[layer],
                     device(to_y, x_lo, to_core),
@@ -307,15 +345,16 @@
             @pl.when(core == to_core)
             def _():
                 pltpu.make_async_copy(
-                    x1.at[layer, rows, cut(y, HD)], x2.at[layer, mine, at, :], x2_recv.at[layer]
+                    x1.at[layer, to_core, :, cut(y, HD)], target, x2_recv.at[layer]
                 ).start()
 
             return carry
 
         lax.fori_loop(0, LAYERS, one, 0)
 
-    for part in PARTS[:2]:
-        pass_x(part)
+    pass_x(0)
+    each(1, N_SEC + 1, pass_z)
+    pass_x(1)
 
     for n, ref in enumerate((k2, v2)):
         wait_for(ref.at[core], recv.at[4 + n])
@@ -323,9 +362,6 @@
             ref.at[core], ref.at[core], send.at[6 + n], recv.at[6 + n], device(y, x_lo, other)
         ).start()
     lax.fori_loop(0, N_CTX, make_bias, 0)
-    for part in PARTS[2:]:
-        pass_x(part)
-
     wait_for(top2, recv.at[3])
     in_order(top2, ranks, g_ref, ROWS, F32)
     dk_ref[...] = jnp.zeros_like(dk_ref)
@@ -362,7 +398,8 @@
 
     def one_layer(step, carry):
         layer = LAYERS - 1 - step
-        wait_for(x2.at[layer], x2_recv.at[layer])
+        wait_for(x2.at[layer, :, pl.ds(0, PART), :], x2_recv.at[layer])
+        wait_for(x2.at[layer, :, pl.ds(PART, PART), :], z2_recv.at[layer])
         in_order(x2.at[layer], ranks, xw, ROWS, F32)
         xf = xw[...]
         gain = gain1[layer]
@@ -497,6 +534,8 @@
     for n, ref in enumerate((k1, v1)):
         wait_for(ref.at[pl.ds(0, TOK_DEV - TOK_SEC), :], send.at[n])
     wait_for(x1.at[most], send.at[2])
+    wait_for(z1.at[:, most], send.at[14])
+    wait_for(z1.at[most], send.at[15])
     wait_for(top2.at[most], send.at[3])
     for n, ref in enumerate((k2, v2)):
         wait_for(ref.at[0, most], send.at[4 + n])
@@ -507,7 +546,7 @@
         wait_for(part5.at[pl.ds(0, TOK_DEV - TOK_SEC), :], send.at[12 + n])
 
     def left(layer, carry):
-        wait_for(x2.at[layer, most], x2_send.at[layer])
+        wait_for(x2.at[layer, most, pl.ds(0, PART), :], x2_send.at[layer])
         wait_for(g1.at[layer, most], g1_send.at[layer])
 
         @pl.when(layer != s)
@@ -519,6 +558,28 @@
     lax.fori_loop(0, LAYERS, left, 0)
     for k in range(1, N_SEC):
         wait_for(gain1.at[0], gain_send.at[k])
+
+
+def widen_kernel(*refs):
+    for source, target in zip(refs[:3], refs[3:]):
+        target[...] = source[...].astype(F32)
+
+
+def widen(*values):
+    def block(value):
+        lead = value.shape[:-1]
+        return pl.BlockSpec(
+            (*lead, WIDTH // WIDEN_STEPS), lambda n, zeros=(0,) * len(lead): (*zeros, n)
+        )
+
+    specs = [block(value) for value in values]
+    return pl.pallas_call(
+        widen_kernel,
+        grid=(WIDEN_STEPS,),
+        out_shape=tuple(jax.ShapeDtypeStruct(value.shape, F32) for value in values),
+        in_specs=specs,
+        out_specs=tuple(specs),
+    )(*values)
 
 
 def body(x_saved, gains, keys, values, grad_top, block_order):
@@ -537,7 +598,8 @@
         scratch_shapes=[
             pltpu.VMEM((TOK_DEV, WIDE), BF16),
             pltpu.VMEM((TOK_DEV, WIDE), BF16),
-            pltpu.VMEM((LAYERS, TOK_DEV, WIDE), BF16),
+            pltpu.VMEM((LAYERS, 2, PART, WIDE), BF16),
+            pltpu.VMEM((N_SEC, N_NEAR, PART, HD), BF16),
             pltpu.VMEM((LAYERS, 1, HD), F32),
             pltpu.VMEM((N_NEAR, ROWS, HD), BF16),
             pltpu.VMEM((2, N_NEAR, TOK_DEV, HD), BF16),
@@ -559,12 +621,14 @@
         + [pltpu.VMEM((N_NEAR, TOK_DEV, HD), BF16)] * 8
         + [pltpu.VMEM((TOK_DEV, WIDE), BF16)] * 2
         + [
-            dma((14,)),
+            dma((16,)),
             dma((15,)),
             dma((N_SEC,)),
             dma((N_SEC,)),
-            dma((LAYERS, TOK_DEV // PART)),
+            dma((LAYERS, 2)),
             dma((LAYERS,)),
+            dma((LAYERS,)),
+            dma((N_SEC,)),
             dma((LAYERS,)),
             dma((LAYERS,)),
             dma((LAYERS,)),
@@ -574,7 +638,7 @@
             vmem_limit_bytes=56 * 2**20, collective_id=0, has_side_effects=True
         ),
     )(block_order, x_saved, gains, keys, values, grad_top)
-    return (grads.astype(F32)[None], dk.astype(F32), dv.astype(F32))
+    return widen(grads[None], dk, dv)
 
 
 def solution(mesh):

time: 93.9 us -> 86.1 us (0.917)
  other arithmetic: 4.24 us -> 0 us
  Pallas kernels: 88.8 us -> 85.2 us
    pallas_call x1, Pallas kernels: 88.8 us -> 81.6 us  [body(): pl.pallas_call(kernel, out_shape=(jax.ShapeDtypeStruct((TOK_DEV, WIDTH),...]
    pallas_call x0 -> x1, Pallas kernels: none -> 3.68 us  [widen(): pl.pallas_call(widen_kernel, grid=(WIDEN_STEPS,), out_shape=tuple((jax.Sh...]
    broadcast_in_dim x1 -> x0, other arithmetic: 2.8 us -> none  [body(): return (grads.astype(F32)[None], dk.astype(F32), dv.astype(F32))]
    convert_element_type x2 -> x0, other arithmetic: 1.44 us -> none  [body(): return (grads.astype(F32)[None], dk.astype(F32), dv.astype(F32))]
where the time goes in v4:
time: 86.1 us; the launch traced here: 85.9 us
  Pallas kernels  85.2 us (99%)
    pallas_call x1, Pallas kernels, body(): pl.pallas_call(kernel, out_shape=(jax.ShapeDtypeStruct((TOK_DEV, WIDTH),...  81.6 us
    pallas_call x1, Pallas kernels, widen(): pl.pallas_call(widen_kernel, grid=(WIDEN_STEPS,), out_shape=tuple((jax.Sh...  3.68 us

profile of v4, /device:TPU:1, one launch (start us, length us, event | category | flops | bytes accessed | tf_op | source)
XLA Modules:
  0.0 85.9 jit_solution(1490810132448383307)
XLA Ops:
  0.6 81.6 %shard_map.85 = (bf16[128,4096]{1,0:T(8,128)(2,1)}, bf16[16,4096]{1,0:T(8,128)(2,1)}, bf16[16,4096]{1,0:T(8,128)(2,1)}) custom-call(s32[16]{0:T(128)} %place_ref.1, bf16[1,128,4096]{2,1,0:T(8,128)(2,1)} %x_hbm.1, f32[1,4096]{1,0:T(1,128)} %gain_hbm.1, bf16[16,4096]{1,0:T(8,128)(2,1)} %keys_hbm.1, bf16[16,4096]{1,0:T(8,128)(2,1)} %values_hbm.1, ...), custom_call_target="tpu_custom_call" | custom-call | tf_op jit(solution)/shard_map/pallas_call | solution.py:589
  82.2 3.7 %shard_map.86 = (f32[1,128,4096]{2,1,0:T(8,128)}, f32[16,4096]{1,0:T(8,128)}, f32[16,4096]{1,0:T(8,128)}) custom-call(bf16[1,128,4096]{2,1,0:T(8,128)(2,1)} %bitcast.1, bf16[16,4096]{1,0:T(8,128)(2,1)} %get-tuple-element.7.refs_1_, bf16[16,4096]{1,0:T(8,128)(2,1)} %get-tuple-element.8.refs_2_), custom_call_target="tpu_custom_call" | custom-call | tf_op jit(solution)/shard_map/pallas_call | solution.py:576

commit v5 on v4

--- a/solution.py
+++ b/solution.py
@@ -30,8 +30,7 @@
     (slice(1536, 1792), 256),
     (slice(1792, 2048), 384),
 )
-LAG = 2
-WIDEN_STEPS = 4
+WIDEN_STEPS = 2
 
 masked_score = -1e30
 norm_eps = 1e-06
@@ -104,7 +103,6 @@
     dk_ref,
     dv_ref,
     g1,
-    y1,
     dk1,
     dv1,
     dk2,
@@ -125,8 +123,6 @@
     z1_recv,
     z2_recv,
     g1_send,
-    g1_recv,
-    g2_send,
 ):
     c, s = lax.axis_index("ctx"), lax.axis_index("section")
     y, x_lo, core = c // 4, (c // 2) % 2, c % 2
@@ -168,6 +164,33 @@
     each(1, 4, lambda k: greet(device((y + k) % 4, x_lo, core)))
     each(0, 4, lambda k: greet(device((y + k) % 4, x_lo, other)))
     each(0, 4, lambda k: greet(device((y + k) % 4, 1 - x_lo, core)))
+
+    places = [place_ref[b] for b in range(N_CTX)]
+    near_places = [place_ref[(e // 2) * 4 + x_lo * 2 + e % 2] for e in range(N_NEAR)]
+    ranks = []
+    for e in range(N_NEAR):
+        rank = 0
+        for f in range(N_NEAR):
+            if f != e:
+                rank = rank + jnp.where(near_places[f] < near_places[e], 1, 0)
+        ranks.append(rank)
+
+    def in_order(ref, numbers, target, size, kind):
+        blocks = [(number, ref[n]) for n, number in enumerate(numbers)]
+        for p in range(len(numbers)):
+            target[p * size : (p + 1) * size, :] = pick(p, blocks).astype(kind)
+
+    lane = lax.broadcasted_iota(jnp.int32, (1, NQ), 1)
+    query_at = core * ROWS + lane % ROWS
+    for e in range(N_NEAR):
+        query_at = query_at + jnp.where(lane // ROWS == ranks[e], near_places[e] * TOK_DEV, 0)
+
+    def make_bias(n, carry):
+        key_at = lax.broadcasted_iota(jnp.int32, (TOK_DEV, NQ), 0) + n * TOK_DEV
+        bias_ref[cut(n, TOK_DEV), :] = jnp.where(key_at <= query_at, 0.0, masked_score)
+        return carry
+
+    lax.fori_loop(0, N_CTX, make_bias, 0)
     pl.semaphore_wait(barrier, N_SEC - 1 + 11)
 
     first_hop = ((keys_hbm, k1), (values_hbm, v1))
@@ -262,31 +285,6 @@
         top_hbm.at[cut(core, ROWS), cut(s * HEADS_SEC + y, HD)], top2.at[mine], recv.at[3]
     ).start()
 
-    places = [place_ref[b] for b in range(N_CTX)]
-    near_places = [place_ref[(e // 2) * 4 + x_lo * 2 + e % 2] for e in range(N_NEAR)]
-    ranks = []
-    for e in range(N_NEAR):
-        rank = 0
-        for f in range(N_NEAR):
-            if f != e:
-                rank = rank + jnp.where(near_places[f] < near_places[e], 1, 0)
-        ranks.append(rank)
-
-    def in_order(ref, numbers, target, size, kind):
-        blocks = [(number, ref[n]) for n, number in enumerate(numbers)]
-        for p in range(len(numbers)):
-            target[p * size : (p + 1) * size, :] = pick(p, blocks).astype(kind)
-
-    lane = lax.broadcasted_iota(jnp.int32, (1, NQ), 1)
-    query_at = core * ROWS + lane % ROWS
-    for e in range(N_NEAR):
-        query_at = query_at + jnp.where(lane // ROWS == ranks[e], near_places[e] * TOK_DEV, 0)
-
-    def make_bias(n, carry):
-        key_at = lax.broadcasted_iota(jnp.int32, (TOK_DEV, NQ), 0) + n * TOK_DEV
-        bias_ref[cut(n, TOK_DEV), :] = jnp.where(key_at <= query_at, 0.0, masked_score)
-        return carry
-
     second_hop = ((k1, k2), (v1, v2))
     wait_for(k1, recv.at[0])
     wait_for(v1, recv.at[1])
@@ -361,7 +359,6 @@
         away(
             ref.at[core], ref.at[core], send.at[6 + n], recv.at[6 + n], device(y, x_lo, other)
         ).start()
-    lax.fori_loop(0, N_CTX, make_bias, 0)
     wait_for(top2, recv.at[3])
     in_order(top2, ranks, g_ref, ROWS, F32)
     dk_ref[...] = jnp.zeros_like(dk_ref)
@@ -378,23 +375,6 @@
     for n in range(4):
         rows = slice(n * 512, (n + 1) * 512)
         kt_ref[:, rows] = jnp.transpose(k_ref[rows, :])
-
-    def send_g2(layer):
-        wait_for(y1.at[layer], g1_recv.at[layer])
-
-        @pl.when(layer != s)
-        def _():
-            away(
-                y1.at[layer],
-                grads_out.at[:, cut(s, WIDE)],
-                g2_send.at[layer],
-                recv.at[8],
-                (c, layer),
-            ).start()
-
-        @pl.when(layer == s)
-        def _():
-            pltpu.make_async_copy(y1.at[layer], grads_out.at[:, cut(s, WIDE)], recv.at[8]).start()
 
     def one_layer(step, carry):
         layer = LAYERS - 1 - step
@@ -444,24 +424,27 @@
         for e in range(N_NEAR):
             g1[layer, e] = pick(ranks[e], by_rank)
 
-        def send_g1(to_y, to_core):
+        target = grads_out.at[cut(core, ROWS), cut(s * HEADS_SEC + y, HD)]
+
+        def send_g(to_y, to_core):
             away(
                 g1.at[layer, to_y * 2 + to_core],
-                y1.at[layer, cut(core, ROWS), cut(y, HD)],
+                target,
                 g1_send.at[layer],
-                g1_recv.at[layer],
-                device(to_y, x_lo, to_core),
+                recv.at[8],
+                (to_y * 4 + x_lo * 2 + to_core, layer),
             ).start()
 
-        each(1, 4, lambda k: send_g1((y + k) % 4, core))
-        each(0, 4, lambda k: send_g1((y + k) % 4, other))
-        pltpu.make_async_copy(
-            g1.at[layer, mine], y1.at[layer, cut(core, ROWS), cut(y, HD)], g1_recv.at[layer]
-        ).start()
-
-        @pl.when(step >= LAG)
+        each(1, 4, lambda k: send_g((y + k) % 4, core))
+        each(0, 4, lambda k: send_g((y + k) % 4, other))
+
+        @pl.when(layer != s)
         def _():
-            send_g2(layer + LAG)
+            send_g(y, core)
+
+        @pl.when(layer == s)
+        def _():
+            pltpu.make_async_copy(g1.at[layer, mine], target, recv.at[8]).start()
 
         return carry
 
@@ -502,9 +485,6 @@
         each(0, 4, lambda k: send_sum((y + k) % 4, 1 - x_lo))
         each(1, 4, lambda k: send_sum((y + k) % 4, x_lo))
         pltpu.make_async_copy(part3.at[near], part4.at[near], recv.at[11 + n]).start()
-
-    for layer in range(LAG - 1, -1, -1):
-        send_g2(layer)
 
     for n, (_, _, _, _, part4, part5, out) in enumerate(sums):
         wait_for(part4, recv.at[11 + n])
@@ -547,11 +527,14 @@
 
     def left(layer, carry):
         wait_for(x2.at[layer, most, pl.ds(0, PART), :], x2_send.at[layer])
-        wait_for(g1.at[layer, most], g1_send.at[layer])
 
         @pl.when(layer != s)
         def _():
-            wait_for(y1.at[layer], g2_send.at[layer])
+            wait_for(g1.at[layer], g1_send.at[layer])
+
+        @pl.when(layer == s)
+        def _():
+            wait_for(g1.at[layer, most], g1_send.at[layer])
 
         return carry
 
@@ -616,7 +599,6 @@
             pltpu.VMEM((NK, HD), F32),
             pltpu.VMEM((NK, HD), F32),
             pltpu.VMEM((LAYERS, N_NEAR, ROWS, HD), BF16),
-            pltpu.VMEM((LAYERS, TOK_DEV, WIDE), BF16),
         ]
         + [pltpu.VMEM((N_NEAR, TOK_DEV, HD), BF16)] * 8
         + [pltpu.VMEM((TOK_DEV, WIDE), BF16)] * 2
@@ -629,8 +611,6 @@
             dma((LAYERS,)),
             dma((LAYERS,)),
             dma((N_SEC,)),
-            dma((LAYERS,)),
-            dma((LAYERS,)),
             dma((LAYERS,)),
             dma((LAYERS,)),
         ],

time: 86.1 us -> 82.2 us (0.955)
  Pallas kernels: 85.2 us -> 81.3 us
    pallas_call x1, Pallas kernels: 81.6 us -> 78.6 us  [body(): pl.pallas_call(kernel, out_shape=(jax.ShapeDtypeStruct((TOK_DEV, WIDTH),...]
    pallas_call x1, Pallas kernels: 3.68 us -> 2.63 us  [widen(): pl.pallas_call(widen_kernel, grid=(WIDEN_STEPS,), out_shape=tuple((jax.Sh...]
where the time goes in v5:
time: 82.2 us; the launch traced here: 81.9 us
  Pallas kernels  81.3 us (99%)
    pallas_call x1, Pallas kernels, body(): pl.pallas_call(kernel, out_shape=(jax.ShapeDtypeStruct((TOK_DEV, WIDTH),...  78.6 us
    pallas_call x1, Pallas kernels, widen(): pl.pallas_call(widen_kernel, grid=(WIDEN_STEPS,), out_shape=tuple((jax.Sh...  2.63 us

profile of v5, /device:TPU:1, one launch (start us, length us, event | category | flops | bytes accessed | tf_op | source)
XLA Modules:
  0.0 81.9 jit_solution(6512499867827134088)
XLA Ops:
  0.6 78.6 %shard_map.85 = (bf16[128,4096]{1,0:T(8,128)(2,1)}, bf16[16,4096]{1,0:T(8,128)(2,1)}, bf16[16,4096]{1,0:T(8,128)(2,1)}) custom-call(s32[16]{0:T(128)} %place_ref.1, bf16[1,128,4096]{2,1,0:T(8,128)(2,1)} %x_hbm.1, f32[1,4096]{1,0:T(1,128)} %gain_hbm.1, bf16[16,4096]{1,0:T(8,128)(2,1)} %keys_hbm.1, bf16[16,4096]{1,0:T(8,128)(2,1)} %values_hbm.1, ...), custom_call_target="tpu_custom_call" | custom-call | tf_op jit(solution)/shard_map/pallas_call | solution.py:572
  79.3 2.6 %shard_map.86 = (f32[1,128,4096]{2,1,0:T(8,128)}, f32[16,4096]{1,0:T(8,128)}, f32[16,4096]{1,0:T(8,128)}) custom-call(bf16[1,128,4096]{2,1,0:T(8,128)(2,1)} %bitcast.1, bf16[16,4096]{1,0:T(8,128)(2,1)} %get-tuple-element.7.refs_1_, bf16[16,4096]{1,0:T(8,128)(2,1)} %get-tuple-element.8.refs_2_), custom_call_target="tpu_custom_call" | custom-call | tf_op jit(solution)/shard_map/pallas_call | solution.py:559

commit v6 on v5

--- a/solution.py
+++ b/solution.py
@@ -30,6 +30,7 @@
     (slice(1536, 1792), 256),
     (slice(1792, 2048), 384),
 )
+TURNS = 2
 WIDEN_STEPS = 2
 
 masked_score = -1e30
@@ -113,6 +114,8 @@
     dv4,
     dk5,
     dv5,
+    dk6,
+    dv6,
     send,
     recv,
     gain_send,
@@ -376,12 +379,13 @@
         rows = slice(n * 512, (n + 1) * 512)
         kt_ref[:, rows] = jnp.transpose(k_ref[rows, :])
 
-    def one_layer(step, carry):
-        layer = LAYERS - 1 - step
+    def wait_layer(layer):
         wait_for(x2.at[layer, :, pl.ds(0, PART), :], x2_recv.at[layer])
         wait_for(x2.at[layer, :, pl.ds(PART, PART), :], z2_recv.at[layer])
-        in_order(x2.at[layer], ranks, xw, ROWS, F32)
-        xf = xw[...]
+
+    def one_layer(layer, turn):
+        in_order(x2.at[layer], ranks, xw.at[turn], ROWS, F32)
+        xf = xw[turn]
         gain = gain1[layer]
         inv_rms = lax.rsqrt(jnp.mean(xf * xf, axis=1, keepdims=True) + norm_eps)
         query = (xf * inv_rms * gain).astype(BF16)
@@ -390,22 +394,22 @@
         row_max = None
         for rows, first in CHUNKS:
             scores = dot(k_ref[rows, :], query[first:, :], NT) + bias_ref[rows, first:]
-            s_ref[rows, first:] = scores
+            s_ref[turn, rows, first:] = scores
             row_max = max_from(row_max, jnp.max(scores, axis=0, keepdims=True), first)
 
         total = None
         for rows, first in CHUNKS:
-            e = jnp.exp2((s_ref[rows, first:] - row_max[:, first:]) * (factor * log2e))
-            s_ref[rows, first:] = e
+            e = jnp.exp2((s_ref[turn, rows, first:] - row_max[:, first:]) * (factor * log2e))
+            s_ref[turn, rows, first:] = e
             total = add_from(total, jnp.sum(e, axis=0, keepdims=True), first)
         inv_total = 1.0 / total
 
         delta = None
         for rows, first in CHUNKS:
             dp = dot(v_ref[rows, :], grad[first:, :], NT)
-            dp_ref[rows, first:] = dp
-            probs = s_ref[rows, first:] * inv_total[:, first:]
-            s_ref[rows, first:] = probs
+            dp_ref[turn, rows, first:] = dp
+            probs = s_ref[turn, rows, first:] * inv_total[:, first:]
+            s_ref[turn, rows, first:] = probs
             low = probs.astype(BF16)
             part = jnp.sum(low.astype(F32) * dp, axis=0, keepdims=True)
             delta = add_from(delta, part, first)
@@ -413,7 +417,7 @@
 
         dq_t = None
         for rows, first in CHUNKS:
-            ds = s_ref[rows, first:] * (dp_ref[rows, first:] - delta[:, first:])
+            ds = s_ref[turn, rows, first:] * (dp_ref[turn, rows, first:] - delta[:, first:])
             ds = ds.astype(BF16)
             dk_ref[rows, :] += dot(ds, query[first:, :], NN)
             dq_t = add_from(dq_t, dot(kt_ref[:, rows], ds, NN), first)
@@ -424,88 +428,109 @@
         for e in range(N_NEAR):
             g1[layer, e] = pick(ranks[e], by_rank)
 
-        target = grads_out.at[cut(core, ROWS), cut(s * HEADS_SEC + y, HD)]
-
-        def send_g(to_y, to_core):
-            away(
-                g1.at[layer, to_y * 2 + to_core],
-                target,
-                g1_send.at[layer],
-                recv.at[8],
-                (to_y * 4 + x_lo * 2 + to_core, layer),
-            ).start()
-
-        each(1, 4, lambda k: send_g((y + k) % 4, core))
-        each(0, 4, lambda k: send_g((y + k) % 4, other))
-
+    target = grads_out.at[cut(core, ROWS), cut(s * HEADS_SEC + y, HD)]
+
+    def send_g(layer, to_y, to_core):
+        away(
+            g1.at[layer, to_y * 2 + to_core],
+            target,
+            g1_send.at[layer],
+            recv.at[8],
+            (to_y * 4 + x_lo * 2 + to_core, layer),
+        ).start()
+
+    def send_layer(layer):
+        for k in range(1, 4):
+            send_g(layer, (y + k) % 4, core)
+        for k in range(4):
+            send_g(layer, (y + k) % 4, other)
+
+    def send_own(layer):
         @pl.when(layer != s)
         def _():
-            send_g(y, core)
+            send_g(layer, y, core)
 
         @pl.when(layer == s)
         def _():
             pltpu.make_async_copy(g1.at[layer, mine], target, recv.at[8]).start()
 
+    def some_layers(step, carry):
+        layers = [LAYERS - 1 - step * TURNS - turn for turn in range(TURNS)]
+        for layer in layers:
+            wait_layer(layer)
+        for turn, layer in enumerate(layers):
+            one_layer(layer, turn % 2)
+        for layer in layers:
+            send_layer(layer)
+            send_own(layer)
         return carry
 
-    lax.fori_loop(0, LAYERS, one_layer, 0)
+    lax.fori_loop(0, LAYERS // TURNS, some_layers, 0)
 
     dk_ref[...] = dk_ref[...] * factor
     sums = (
-        (dk_ref, dk1, dk2, dk3, dk4, dk5, dk_out),
-        (dv_ref, dv1, dv2, dv3, dv4, dv5, dv_out),
+        (dk_ref, dk1, dk2, dk3, dk4, dk5, dk6, dk_out),
+        (dv_ref, dv1, dv2, dv3, dv4, dv5, dv6, dv_out),
     )
 
-    def in_blocks(ref, of_core, kind):
-        by_place = [
-            (p, ref[p * TOK_DEV : (p + 1) * TOK_DEV, :].astype(kind)) for p in range(N_CTX)
-        ]
+    def by_place(ref, kind):
+        return [(p, ref[p * TOK_DEV : (p + 1) * TOK_DEV, :].astype(kind)) for p in range(N_CTX)]
+
+    for n, (ref, part1, part2, _, _, _, _, _) in enumerate(sums):
+        rows = by_place(ref, BF16)
         for f in range(N_NEAR):
-            yield f, pick(place_ref[f * 2 + of_core], by_place)
-
-    for n, (ref, part1, part2, _, _, _, _) in enumerate(sums):
-        for f, rows in in_blocks(ref, other, BF16):
-            part1[f] = rows
+            part1[f] = pick(place_ref[f * 2 + other], rows)
         away(part1, part2, send.at[8 + n], recv.at[9 + n], device(y, x_lo, other)).start()
 
-    for n, (ref, _, part2, part3, part4, _, _) in enumerate(sums):
+    for n, (ref, _, part2, part3, part4, _, _, _) in enumerate(sums):
         wait_for(part2, recv.at[9 + n])
-        for f, rows in in_blocks(ref, core, F32):
-            part3[f] = (rows + part2[f].astype(F32)).astype(BF16)
-
-        def send_sum(to_y, to_x_lo):
-            away(
-                part3.at[to_y * 2 + to_x_lo],
-                part4.at[near],
-                send.at[10 + n],
-                recv.at[11 + n],
-                device(to_y, to_x_lo, core),
-            ).start()
-
-        each(0, 4, lambda k: send_sum((y + k) % 4, 1 - x_lo))
-        each(1, 4, lambda k: send_sum((y + k) % 4, x_lo))
-        pltpu.make_async_copy(part3.at[near], part4.at[near], recv.at[11 + n]).start()
-
-    for n, (_, _, _, _, part4, part5, out) in enumerate(sums):
+        rows = by_place(ref, F32)
+        for to_y in range(4):
+            f = to_y * 2 + 1 - x_lo
+            both = pick(place_ref[f * 2 + core], rows) + part2[f].astype(F32)
+            part3[to_y] = both.astype(BF16)
+        away(
+            part3, part4, send.at[10 + n], recv.at[11 + n], device(y, 1 - x_lo, core)
+        ).start()
+
+    for ref, _, part2, _, _, part5, _, _ in sums:
+        rows = by_place(ref, F32)
+        for to_y in range(4):
+            f = to_y * 2 + x_lo
+            part5[to_y] = pick(place_ref[f * 2 + core], rows) + part2[f].astype(F32)
+
+    for n, (_, _, _, _, part4, part5, part6, out) in enumerate(sums):
         wait_for(part4, recv.at[11 + n])
-        for h in range(HEADS_SEC):
-            both = part4[h * 2].astype(F32) + part4[h * 2 + 1].astype(F32)
-            part5[:, h * HD : (h + 1) * HD] = both.astype(BF16)
-
-        def send_whole(k):
-            to = sec_at(k)
-            away(
-                part5.at[cut(to, TOK_SEC), :],
-                out.at[:, cut(s, WIDE)],
-                send.at[12 + n],
-                recv.at[13 + n],
-                (c, to),
-            ).start()
-
-        each(1, N_SEC, send_whole)
-        pltpu.make_async_copy(
-            part5.at[cut(s, TOK_SEC), :], out.at[:, cut(s, WIDE)], recv.at[13 + n]
-        ).start()
+        for to_y in range(4):
+            total = part5[to_y] + part4[to_y].astype(F32)
+            part6[to_y * TOK_DEV : (to_y + 1) * TOK_DEV, :] = total.astype(BF16)
+        target = out.at[:, cut(s * HEADS_SEC + y, HD)]
+
+        def send_sums(k):
+            to_sec = sec_at(k)
+
+            def send_sum(to_y):
+                away(
+                    part6.at[cut(to_y * N_SEC + to_sec, TOK_SEC), :],
+                    target,
+                    send.at[12 + n],
+                    recv.at[13 + n],
+                    (to_y * 4 + x_lo * 2 + core, to_sec),
+                ).start()
+
+            each(1, 4, lambda q: send_sum((y + q) % 4))
+
+            @pl.when(to_sec != s)
+            def _():
+                send_sum(y)
+
+            @pl.when(to_sec == s)
+            def _():
+                pltpu.make_async_copy(
+                    part6.at[cut(y * N_SEC + s, TOK_SEC), :], target, recv.at[13 + n]
+                ).start()
+
+        each(1, N_SEC + 1, send_sums)
 
     wait_for(grads_out, recv.at[8])
     wait_for(dk_out, recv.at[13])
@@ -520,10 +545,10 @@
     for n, ref in enumerate((k2, v2)):
         wait_for(ref.at[0, most], send.at[4 + n])
         wait_for(ref.at[0], send.at[6 + n])
-    for n, (_, part1, _, part3, _, part5, _) in enumerate(sums):
+    for n, (_, part1, _, part3, _, _, part6, _) in enumerate(sums):
         wait_for(part1, send.at[8 + n])
-        wait_for(part3.at[most], send.at[10 + n])
-        wait_for(part5.at[pl.ds(0, TOK_DEV - TOK_SEC), :], send.at[12 + n])
+        wait_for(part3, send.at[10 + n])
+        wait_for(part6.at[pl.ds(0, 4 * TOK_DEV - TOK_SEC), :], send.at[12 + n])
 
     def left(layer, carry):
         wait_for(x2.at[layer, most, pl.ds(0, PART), :], x2_send.at[layer])
@@ -588,20 +613,22 @@
             pltpu.VMEM((2, N_NEAR, TOK_DEV, HD), BF16),
             pltpu.VMEM((2, N_NEAR, TOK_DEV, HD), BF16),
             pltpu.VMEM((LAYERS, N_NEAR, ROWS, HD), BF16),
-            pltpu.VMEM((NQ, HD), F32),
+            pltpu.VMEM((2, NQ, HD), F32),
             pltpu.VMEM((NK, HD), BF16),
             pltpu.VMEM((NK, HD), BF16),
             pltpu.VMEM((HD, NK), BF16),
             pltpu.VMEM((NK, NQ), F32),
-            pltpu.VMEM((NK, NQ), F32),
-            pltpu.VMEM((NK, NQ), F32),
+            pltpu.VMEM((2, NK, NQ), F32),
+            pltpu.VMEM((2, NK, NQ), F32),
             pltpu.VMEM((NQ, HD), F32),
             pltpu.VMEM((NK, HD), F32),
             pltpu.VMEM((NK, HD), F32),
             pltpu.VMEM((LAYERS, N_NEAR, ROWS, HD), BF16),
         ]
-        + [pltpu.VMEM((N_NEAR, TOK_DEV, HD), BF16)] * 8
-        + [pltpu.VMEM((TOK_DEV, WIDE), BF16)] * 2
+        + [pltpu.VMEM((N_NEAR, TOK_DEV, HD), BF16)] * 4
+        + [pltpu.VMEM((4, TOK_DEV, HD), BF16)] * 4
+        + [pltpu.VMEM((4, TOK_DEV, HD), F32)] * 2
+        + [pltpu.VMEM((4 * TOK_DEV, HD), BF16)] * 2
         + [
             dma((16,)),
             dma((15,)),

time: 82.2 us -> 78.9 us (0.960)
  Pallas kernels: 81.3 us -> 78.1 us
    pallas_call x1, Pallas kernels: 78.6 us -> 75.5 us  [body(): pl.pallas_call(kernel, out_shape=(jax.ShapeDtypeStruct((TOK_DEV, WIDTH),...]
where the time goes in v6:
time: 78.9 us; the launch traced here: 78.8 us
  Pallas kernels  78.1 us (99%)
    pallas_call x1, Pallas kernels, body(): pl.pallas_call(kernel, out_shape=(jax.ShapeDtypeStruct((TOK_DEV, WIDTH),...  75.5 us
    pallas_call x1, Pallas kernels, widen(): pl.pallas_call(widen_kernel, grid=(WIDEN_STEPS,), out_shape=tuple((jax.Sh...  2.63 us

profile of v6, /device:TPU:1, one launch (start us, length us, event | category | flops | bytes accessed | tf_op | source)
XLA Modules:
  0.0 78.8 jit_solution(14737271222188525100)
XLA Ops:
  0.6 75.5 %shard_map.85 = (bf16[128,4096]{1,0:T(8,128)(2,1)}, bf16[16,4096]{1,0:T(8,128)(2,1)}, bf16[16,4096]{1,0:T(8,128)(2,1)}) custom-call(s32[16]{0:T(128)} %place_ref.1, bf16[1,128,4096]{2,1,0:T(8,128)(2,1)} %x_hbm.1, f32[1,4096]{1,0:T(1,128)} %gain_hbm.1, bf16[16,4096]{1,0:T(8,128)(2,1)} %keys_hbm.1, bf16[16,4096]{1,0:T(8,128)(2,1)} %values_hbm.1, ...), custom_call_target="tpu_custom_call" | custom-call | tf_op jit(solution)/shard_map/pallas_call | solution.py:597
  76.2 2.6 %shard_map.86 = (f32[1,128,4096]{2,1,0:T(8,128)}, f32[16,4096]{1,0:T(8,128)}, f32[16,4096]{1,0:T(8,128)}) custom-call(bf16[1,128,4096]{2,1,0:T(8,128)(2,1)} %bitcast.1, bf16[16,4096]{1,0:T(8,128)(2,1)} %get-tuple-element.7.refs_1_, bf16[16,4096]{1,0:T(8,128)(2,1)} %get-tuple-element.8.refs_2_), custom_call_target="tpu_custom_call" | custom-call | tf_op jit(solution)/shard_map/pallas_call | solution.py:584

commit v7 on v6

--- a/solution.py
+++ b/solution.py
@@ -462,19 +462,23 @@
             one_layer(layer, turn % 2)
         for layer in layers:
             send_layer(layer)
+        for layer in layers:
             send_own(layer)
         return carry
 
     lax.fori_loop(0, LAYERS // TURNS, some_layers, 0)
 
-    dk_ref[...] = dk_ref[...] * factor
     sums = (
+        (dv_ref, dv1, dv2, dv3, dv4, dv5, dv6, dv_out),
         (dk_ref, dk1, dk2, dk3, dk4, dk5, dk6, dk_out),
-        (dv_ref, dv1, dv2, dv3, dv4, dv5, dv6, dv_out),
     )
 
     def by_place(ref, kind):
-        return [(p, ref[p * TOK_DEV : (p + 1) * TOK_DEV, :].astype(kind)) for p in range(N_CTX)]
+        scale = factor if ref is dk_ref else 1.0
+        return [
+            (p, (ref[p * TOK_DEV : (p + 1) * TOK_DEV, :] * scale).astype(kind))
+            for p in range(N_CTX)
+        ]
 
     for n, (ref, part1, part2, _, _, _, _, _) in enumerate(sums):
         rows = by_place(ref, BF16)
@@ -533,8 +537,8 @@
         each(1, N_SEC + 1, send_sums)
 
     wait_for(grads_out, recv.at[8])
-    wait_for(dk_out, recv.at[13])
-    wait_for(dv_out, recv.at[14])
+    wait_for(dv_out, recv.at[13])
+    wait_for(dk_out, recv.at[14])
     most = pl.ds(0, N_SEC - 1)
     for n, ref in enumerate((k1, v1)):
         wait_for(ref.at[pl.ds(0, TOK_DEV - TOK_SEC), :], send.at[n])

time: 78.9 us -> 78.7 us (level)
  no operation moved by 1% of the time
where the time goes in v7:
time: 78.7 us; the launch traced here: 78.5 us
  Pallas kernels  77.9 us (99%)
    pallas_call x1, Pallas kernels, body(): pl.pallas_call(kernel, out_shape=(jax.ShapeDtypeStruct((TOK_DEV, WIDTH),...  75.2 us
    pallas_call x1, Pallas kernels, widen(): pl.pallas_call(widen_kernel, grid=(WIDEN_STEPS,), out_shape=tuple((jax.Sh...  2.63 us

profile of v7, /device:TPU:1, one launch (start us, length us, event | category | flops | bytes accessed | tf_op | source)
XLA Modules:
  0.0 78.5 jit_solution(2717926828797489956)
XLA Ops:
  0.6 75.2 %shard_map.85 = (bf16[128,4096]{1,0:T(8,128)(2,1)}, bf16[16,4096]{1,0:T(8,128)(2,1)}, bf16[16,4096]{1,0:T(8,128)(2,1)}) custom-call(s32[16]{0:T(128)} %place_ref.1, bf16[1,128,4096]{2,1,0:T(8,128)(2,1)} %x_hbm.1, f32[1,4096]{1,0:T(1,128)} %gain_hbm.1, bf16[16,4096]{1,0:T(8,128)(2,1)} %keys_hbm.1, bf16[16,4096]{1,0:T(8,128)(2,1)} %values_hbm.1, ...), custom_call_target="tpu_custom_call" | custom-call | tf_op jit(solution)/shard_map/pallas_call | solution.py:601
  75.9 2.6 %shard_map.86 = (f32[1,128,4096]{2,1,0:T(8,128)}, f32[16,4096]{1,0:T(8,128)}, f32[16,4096]{1,0:T(8,128)}) custom-call(bf16[1,128,4096]{2,1,0:T(8,128)(2,1)} %bitcast.1, bf16[16,4096]{1,0:T(8,128)(2,1)} %get-tuple-element.7.refs_1_, bf16[16,4096]{1,0:T(8,128)(2,1)} %get-tuple-element.8.refs_2_), custom_call_target="tpu_custom_call" | custom-call | tf_op jit(solution)/shard_map/pallas_call | solution.py:588
